TPU v7x, 256 devices: a whole 4x4x8 slice. The times are simulated.
256 devices in a mesh: dp: 16 (over z, x_hi), tensor: 16 (over y, x_lo, core).
Axes of the slice: x: 4 (x_hi: 2, x_lo: 2; x = x_hi * 2 + x_lo), y: 4, z: 8, core: 2. Of those that a mesh axis runs over, the one named last changes fastest.
Arguments:
- patches: bfloat16 [512, 256, 6144], P('dp', None, 'tensor'), may hold values from -6 to 6
- visible: int32 [512, 64], P('dp'), may hold values from 0 to 255, as said below
- block_perm: int32 [64], replicated, may hold values from 0 to 63, each once
- first_left: bfloat16 [64, 96, 96], P('tensor', 'dp'), may hold values from -0.625 to 0.625
- first_right: bfloat16 [96, 64, 256], P('tensor', 'dp'), may hold values from -0.75 to 0.75
- second_right: bfloat16 [96, 256, 64], P('tensor', 'dp'), may hold values from -0.375 to 0.375
- second_left: bfloat16 [64, 96, 96], P('tensor', 'dp'), may hold values from -0.625 to 0.625
- cotangent: bfloat16 [32768, 6144], P('dp', 'tensor'), may hold values from -6 to 6
Outputs:
- mlp_out: bfloat16 [32768, 6144], P('dp', 'tensor')
- token_grad: bfloat16 [32768, 6144], P('dp', 'tensor')
- grad_first_left: float32 [64, 96, 96], P('tensor', 'dp')
- grad_first_right: float32 [96, 64, 256], P('tensor', 'dp')
- grad_second_right: float32 [96, 256, 64], P('tensor', 'dp')
- grad_second_left: float32 [64, 96, 96], P('tensor', 'dp')
Inputs may be any that keep to these rules, and one draw needn't show every extreme that they name: `visible`: each row holds 64 different patch indices in increasing order. `block_perm`: each block number appears once.
All inputs are finite; a program needn't handle non-finite values.
Results may differ from a plain program's by a relative error of at most 0.022.
Values may be sent and summed in bfloat16 or wider, within the bound.
No kernel may reach another device: no remote copies, remote signals or barrier semaphores. Data moves between devices by JAX's collectives and lax.ppermute only.
A program may use at most 128 MiB of HBM per device.

v0:
```python
import math

import jax
import jax.numpy as jnp
from jax import lax
from jax.sharding import PartitionSpec as P

NB = 64
BS = 96


root_ratio = math.sqrt(2.0 / math.pi)


def gelu_value(hidden):
    inner = root_ratio * (hidden + 0.044715 * hidden * hidden * hidden)
    return 0.5 * hidden * (1.0 + jnp.tanh(inner))


def gelu_slope(hidden):
    inner = root_ratio * (hidden + 0.044715 * hidden * hidden * hidden)
    tangent = jnp.tanh(inner)
    return 0.5 * (1.0 + tangent) + 0.5 * hidden * (1.0 - tangent * tangent) * root_ratio * (
        1.0 + 3.0 * 0.044715 * hidden * hidden
    )


def mix_forward(arrived, right_ordered, down_ordered):
    hidden = jnp.einsum("ptb,pbk->ptk", arrived, right_ordered, preferred_element_type=jnp.float32)
    activated = gelu_value(hidden).astype(jnp.bfloat16)
    leaving = jnp.einsum(
        "ptk,pkb->ptb", activated, down_ordered, preferred_element_type=jnp.float32
    ).astype(jnp.bfloat16)
    return (hidden, activated, leaving)


def mix_backward(arrived_grad, block_perm, arrived, hidden, activated, right_ordered, down_ordered):
    grad_act = jnp.einsum(
        "ptb,pkb->ptk", arrived_grad, down_ordered, preferred_element_type=jnp.float32
    )
    block_two = jnp.einsum(
        "ptk,ptb->pkb", activated, arrived_grad, preferred_element_type=jnp.float32
    )
    grad_right_two = jnp.take(block_two, block_perm, axis=2)
    grad_hidden = (grad_act * gelu_slope(hidden)).astype(jnp.bfloat16)
    leaving_grad = jnp.einsum(
        "ptk,pbk->ptb", grad_hidden, right_ordered, preferred_element_type=jnp.float32
    ).astype(jnp.bfloat16)
    block_one = jnp.einsum("ptb,ptk->pbk", arrived, grad_hidden, preferred_element_type=jnp.float32)
    grad_right_one = jnp.take(block_one, block_perm, axis=1)
    return (leaving_grad, grad_right_one, grad_right_two)


def local(
    patches, visible, block_perm, first_left, first_right, second_right, second_left, cotangent
):
    feature_count = patches.shape[2]
    local_blocks = feature_count // BS
    picked = jnp.take_along_axis(patches, visible[:, :, None], axis=1)
    tokens = picked.reshape(-1, local_blocks, BS)
    upstream = cotangent.reshape(-1, local_blocks, BS)
    inverse = jnp.zeros_like(block_perm).at[block_perm].set(jnp.arange(NB, dtype=jnp.int32))
    left_one = lax.all_gather(first_left, "dp", axis=1, tiled=True)
    right_one = lax.all_gather(first_right, "dp", axis=1, tiled=True)
    right_two = lax.all_gather(second_right, "dp", axis=1, tiled=True)
    left_two = lax.all_gather(second_left, "dp", axis=1, tiled=True)
    right_ordered = jnp.take(right_one, inverse, axis=1)
    down_ordered = jnp.take(right_two, inverse, axis=2)
    section_one = jnp.einsum(
        "tbi,bij->jtb", tokens, left_one, preferred_element_type=jnp.float32
    ).astype(jnp.bfloat16)
    back_grad = jnp.einsum(
        "tbj,bij->itb", upstream, left_two, preferred_element_type=jnp.float32
    ).astype(jnp.bfloat16)
    arrived = lax.all_to_all(section_one, "tensor", split_axis=0, concat_axis=2, tiled=True)
    hidden, activated, leaving = mix_forward(arrived, right_ordered, down_ordered)
    returned = lax.all_to_all(leaving, "tensor", split_axis=2, concat_axis=0, tiled=True)
    arrived_grad = lax.all_to_all(back_grad, "tensor", split_axis=0, concat_axis=2, tiled=True)
    leaving_grad, grad_right_one, grad_right_two = mix_backward(
        arrived_grad, block_perm, arrived, hidden, activated, right_ordered, down_ordered
    )
    returned_grad = lax.all_to_all(leaving_grad, "tensor", split_axis=2, concat_axis=0, tiled=True)
    output = jnp.einsum(
        "itb,bij->tbj", returned, left_two, preferred_element_type=jnp.float32
    ).astype(jnp.bfloat16)
    grad_left_two = jnp.einsum(
        "itb,tbj->bij", returned, upstream, preferred_element_type=jnp.float32
    )
    grad_left_one = jnp.einsum(
        "tbi,jtb->bij", tokens, returned_grad, preferred_element_type=jnp.float32
    )
    token_grad = jnp.einsum(
        "jtb,bij->tbi", returned_grad, left_one, preferred_element_type=jnp.float32
    ).astype(jnp.bfloat16)
    share_left_one = lax.psum_scatter(
        grad_left_one.astype(jnp.bfloat16), "dp", scatter_dimension=1, tiled=True
    ).astype(jnp.float32)
    share_right_one = lax.psum_scatter(
        grad_right_one.astype(jnp.bfloat16), "dp", scatter_dimension=1, tiled=True
    ).astype(jnp.float32)
    share_right_two = lax.psum_scatter(
        grad_right_two.astype(jnp.bfloat16), "dp", scatter_dimension=1, tiled=True
    ).astype(jnp.float32)
    share_left_two = lax.psum_scatter(
        grad_left_two.astype(jnp.bfloat16), "dp", scatter_dimension=1, tiled=True
    ).astype(jnp.float32)
    return (
        output.reshape(-1, feature_count),
        token_grad.reshape(-1, feature_count),
        share_left_one,
        share_right_one,
        share_right_two,
        share_left_two,
    )


def solution(mesh):
    placed = (
        P("dp", None, "tensor"),
        P("dp", None),
        P(),
        P("tensor", "dp", None),
        P("tensor", "dp", None),
        P("tensor", "dp", None),
        P("tensor", "dp", None),
        P("dp", "tensor"),
    )
    return jax.shard_map(
        local,
        mesh=mesh,
        in_specs=placed,
        out_specs=(
            P("dp", "tensor"),
            P("dp", "tensor"),
            P("tensor", "dp", None),
            P("tensor", "dp", None),
            P("tensor", "dp", None),
            P("tensor", "dp", None),
        ),
        check_vma=False,
    )
```

profile of v0, /device:TPU:2, one launch (start us, length us, event | category | flops | bytes accessed | tf_op | source)
XLA Modules:
  0.0 898.1 jit_solution(12693317402725394410)
XLA Ops:
  7.2 0.7 bitcast_or_fusion
  8.7 27.0 %gather_fusion.4 = bf16[2048,384]{1,0:T(8,128)(2,1)S(1)} fusion(bf16[32,256,384]{2,1,0:T(8,128)(2,1)} %param.8, s32[2048]{0:T(1024)S(1)} %reshape.78), kind=kCustom, calls=%fused_computation.4 | custom fusion | bytes 3162112 | tf_op jit(solution)/shard_map/jit(take_along_axis)/gather | solution.py:59
  35.7 0.8 copy.60
  36.5 43.4 %all_gather.12 = bf16[4,96,96]{2,0,1:T(4,128)(2,1)S(1)} all-gather(bf16[4,6,96]{2,0,1:T(4,128)(2,1)S(1)} %copy-done.16), channel_id=1, replica_groups=mesh['dp'=16,'tensor'=16] {'dp'}, dimensions={1}, use_global_device_ids=true | all-gather | bytes 78336 | tf_op jit(solution)/shard_map/all_gather | solution.py:63
  80.7 2.4 copy.62
  83.0 6.0 all-to-all-start
  89.1 1.7 copy.72
  90.8 49.4 %all_gather.15 = bf16[4,96,96]{2,0,1:T(4,128)(2,1)S(1)} all-gather(bf16[4,6,96]{2,0,1:T(4,128)(2,1)S(1)} %copy-done.17), channel_id=1, replica_groups=mesh['dp'=16,'tensor'=16] {'dp'}, dimensions={1}, use_global_device_ids=true | all-gather | bytes 78336 | tf_op jit(solution)/shard_map/all_gather | solution.py:66
  140.8 2.4 copy.74
  143.2 5.6 all-to-all-start.2
  148.8 56.4 %all_gather.14 = bf16[6,256,64]{2,1,0:T(8,128)(2,1)} all-gather(bf16[6,16,64]{2,1,0:T(8,128)(2,1)S(1)} %copy-done.14), channel_id=1, replica_groups=mesh['dp'=16,'tensor'=16] {'dp'}, dimensions={1}, use_global_device_ids=true | all-gather | bytes 208896 | tf_op jit(solution)/shard_map/all_gather | solution.py:65
  205.2 1.2 copy.66
  206.6 0.8 scatter_custom_fusion
  207.4 1.3 gather_fusion.1
  208.7 37.2 %all_gather.13 = bf16[6,64,256]{2,0,1:T(8,128)(2,1)S(1)} all-gather(bf16[6,4,256]{2,0,1:T(8,128)(2,1)S(1)} %copy.64), channel_id=1, replica_groups=mesh['dp'=16,'tensor'=16] {'dp'}, dimensions={1}, use_global_device_ids=true | all-gather | bytes 208896 | tf_op jit(solution)/shard_map/all_gather | solution.py:64
  245.8 1.3 gather_fusion
  247.2 1.9 select_bitcast_fusion
  249.0 2.1 copy.63
  251.1 2.3 all_to_all.55
  253.5 2.1 copy.75
  255.6 2.3 all_to_all.63
  258.0 7.5 multiply_convert_fusion
  265.4 9.1 %fusion.6 = bf16[6,2048,256]{2,1,0:T(8,128)(2,1)S(1)} fusion(f32[6,2048,256]{2,1,0:T(8,128)S(1)} %get-tuple-element.31, bf16[6,2048,64]{1,2,0:T(8,128)(2,1)S(1)} %all_to_all.63, bf16[6,256,64]{1,0,2:T(8,128)(2,1)S(1)} %get-tuple-element.28), kind=kOutput, calls=%fused_computation.14 | convolution fusion | flops 462422016 | bytes 20643840 | tf_op jit(solution)/shard_map/ptb,pkb->ptk/dot_general | solution.py:38
  274.6 2.0 convolution_convert_fusion
  277.2 2.2 copy.78
  279.4 5.3 all-to-all-start.3
  284.8 4.9 convolution_convert_fusion.1
  289.7 2.2 copy.68
  292.0 1.1 fusion.38
  294.1 1.1 fusion.39
  296.6 14.9 %all-to-all-done.3 = bf16[6,2048,64]{1,0,2:T(8,128)(2,1)} async-done(((bf16[6,2048,64]{1,0,2:T(8,128)(2,1)}), bf16[6,2048,64]{1,0,2:T(8,128)(2,1)}, u32[]{:S(2)}, u32[]{:S(2)}) %all-to-all-start.3) | async-done | bytes 1572896 | tf_op jit(solution)/shard_map/all_to_all | solution.py:82
  311.5 4.9 all-to-all-start.1
  316.4 0.9 fusion.24
  317.4 1.2 copy.86
  320.9 198.8 %reduce-scatter.5.cloned.1.call-done = bf16[6,16,64]{2,0,1:T(8,128)(2,1)} async-done(((bf16[6,256,64]{2,0,1:T(8,128)(2,1)}), bf16[6,16,64]{2,0,1:T(8,128)(2,1)}) %reduce-scatter.5.cloned.1.call-update) | async-done | bytes 12304 | tf_op jit(solution)/shard_map/reduce_scatter | solution.py:101
  519.6 1.4 copy.92
  521.0 201.5 %reduce-scatter.3.cloned.1.call-done = bf16[6,4,256]{2,0,1:T(8,128)(2,1)} async-done(((bf16[6,64,256]{2,0,1:T(8,128)(2,1)}), bf16[6,4,256]{2,0,1:T(8,128)(2,1)}) %reduce-scatter.3.cloned.1.call-update) | async-done | bytes 12304 | tf_op jit(solution)/shard_map/reduce_scatter | solution.py:98
  722.5 1.3 copy.91
  723.8 3.1 copy.79
  726.9 1.2 fusion.18
  728.7 3.2 convolution_convert_fusion.2
  731.9 1.3 copy.69
  733.3 1.1 fusion.15
  735.2 3.6 convolution_convert_fusion.4
  738.8 1.6 copy.90
  740.4 1.6 copy.89
  741.9 148.3 %all-reduce.5.cloned.1.call-done = (bf16[4,96,96]{2,0,1:T(4,128)(2,1)}, bf16[4,96,96]{2,0,1:T(4,128)(2,1)}) async-done(((bf16[4,96,96]{2,0,1:T(4,128)(2,1)}, bf16[4,96,96]{2,0,1:T(4,128)(2,1)}), (bf16[4,96,96]{2,0,1:T(4,128)(2,1)}, bf16[4,96,96]{2,0,1:T(4,128)(2,1)})) %all-reduce.5.cloned.1.call-update) | async-done | bytes 147472
  890.3 1.3 dynamic-slice_convert_fusion
  (79 shorter events, 8.3 us)
Async XLA Ops:
  35.7 0.8 copy-start.16
  36.5 44.2 %copy-start.9 = (bf16[2048,384]{0,1:T(8,128)(2,1)}, bf16[2048,384]{0,1:T(8,128)(2,1)S(1)}, u32[]{:S(2)}) copy-start(bf16[2048,384]{0,1:T(8,128)(2,1)S(1)} %copy.60) | copy-start | bytes 4718596
  80.0 0.7 copy-start.12
  83.0 60.1 %all-to-all-start = ((bf16[96,2048,4]{1,2,0:T(4,128)(2,1)}), bf16[96,2048,4]{1,2,0:T(4,128)(2,1)S(1)}, u32[]{:S(2)}, u32[]{:S(2)}) async-start(bf16[96,2048,4]{1,2,0:T(4,128)(2,1)} %copy.62), calls=%async_computation | async-start | bytes 3145728 | tf_op jit(solution)/shard_map/all_to_all | solution.py:75
  89.0 1.7 copy-start.17
  90.8 50.0 %copy-start.5 = (bf16[2048,384]{0,1:T(8,128)(2,1)}, bf16[2048,384]{0,1:T(8,128)(2,1)S(1)}, u32[]{:S(2)}) copy-start(bf16[2048,384]{0,1:T(8,128)(2,1)S(1)} %copy.72) | copy-start | bytes 4718596
  143.2 5.6 copy-start.14
  143.2 63.3 %copy-start.15 = (bf16[6,4,256]{2,1,0:T(4,128)(2,1)S(1)}, bf16[6,4,256]{2,1,0:T(4,128)(2,1)}, u32[]{:S(2)}) copy-start(bf16[6,4,256]{2,1,0:T(4,128)(2,1)} %param.12) | copy-start | bytes 36868
  143.2 63.3 %copy-start.18 = (s32[64]{0:T(128)S(1)}, s32[64]{0:T(128)}, u32[]{:S(2)}) copy-start(s32[64]{0:T(128)} %param.10) | copy-start | bytes 772
  143.2 110.3 %all-to-all-start.2 = ((bf16[96,2048,4]{1,2,0:T(4,128)(2,1)}), bf16[96,2048,4]{1,2,0:T(4,128)(2,1)S(1)}, u32[]{:S(2)}, u32[]{:S(2)}) async-start(bf16[96,2048,4]{1,2,0:T(4,128)(2,1)} %copy.74), calls=%async_computation.2 | async-start | bytes 3145728 | tf_op jit(solution)/shard_map/all_to_all | solution.py:78
  253.5 4.5 copy-start.1
  257.9 7.5 copy-start.3
  265.4 9.1 %copy-start.11 = (bf16[6,64,256]{2,0,1:T(8,128)(2,1)S(1)}, bf16[6,64,256]{2,0,1:T(8,128)(2,1)}, u32[]{:S(2)}) copy-start(bf16[6,64,256]{2,0,1:T(8,128)(2,1)} %get-tuple-element.29) | copy-start | bytes 589828
  274.5 2.6 copy-start
  279.4 12.5 %slice-start.2 = ((s8[6291456]{0:T(1024)(128)(4,1)}), s8[2097152]{0:T(1024)(128)(4,1)S(1)}, s32[]{:S(2)}) async-start(s8[6291456]{0:T(1024)(128)(4,1)} %bitcast.55), calls=%async_computation.11 | async-start | bytes 4194304
  279.4 32.1 %all-to-all-start.3 = ((bf16[6,2048,64]{1,0,2:T(8,128)(2,1)}), bf16[6,2048,64]{1,0,2:T(8,128)(2,1)}, u32[]{:S(2)}, u32[]{:S(2)}) async-start(bf16[6,2048,64]{1,0,2:T(8,128)(2,1)} %copy.78), calls=%async_computation.3 | async-start | bytes 4194304 | tf_op jit(solution)/shard_map/all_to_all | solution.py:82
  284.8 7.2 slice-start.3
  284.8 7.2 copy-start.2
  289.7 3.5 slice-start
  291.9 1.8 slice-start.1
  291.9 2.2 copy-start.4
  311.5 420.4 %all-to-all-start.1 = ((bf16[6,2048,64]{1,0,2:T(8,128)(2,1)}), bf16[6,2048,64]{1,0,2:T(8,128)(2,1)S(1)}, u32[]{:S(2)}, u32[]{:S(2)}) async-start(bf16[6,2048,64]{1,0,2:T(8,128)(2,1)} %copy.68), calls=%async_computation.1 | async-start | bytes 4194304 | tf_op jit(solution)/shard_map/all_to_all | solution.py:77
  316.4 3.3 copy-start.19
  316.4 203.2 %reduce-scatter.5.cloned.1.call-start = ((), (), s32[]{:S(2)}) async-start(), calls=%async_computation.7 | async-start | bytes 557056 | tf_op jit(solution)/shard_map/reduce_scatter | solution.py:101
  318.5 403.9 %reduce-scatter.3.cloned.1.call-start = ((), (), s32[]{:S(2)}) async-start(), calls=%async_computation.6 | async-start | bytes 278528 | tf_op jit(solution)/shard_map/reduce_scatter | solution.py:98
  319.3 571.0 %all-reduce.5.cloned.1.call-start = ((), (), s32[]{:S(2)}) async-start(), calls=%async_computation.8 | async-start | bytes 393216
  723.8 3.1 copy-start.10
  726.9 1.9 copy-start.13
  731.9 1.4 copy-start.6
  733.3 1.2 copy-start.8
  735.2 3.6 copy-start.7
Sparse Core Ops, SparseCore 0:
  321.6 197.9 reduce-scatter.4
  524.5 197.9 reduce-scatter.2
  735.3 154.9 all-reduce.4
where the time goes:
time: 900 us; the launch traced here: 898 us
  waiting for transfers between devices  564 us (63%)
  blocking collectives  187 us (21%)
  local copies, waits for them, and re-layouts  68.8 us (8%)
  matrix products  36 us (4%)
  starting transfers between devices  22.2 us (2%)
  between operations  14.8 us (2%)
    reduce_scatter x1, waiting for transfers between devices, local(): lax.psum_scatter(grad_right_one.astype(jnp.bfloat16), 'dp', scatter_dimen...  201 us
    reduce_scatter x1, waiting for transfers between devices, local(): lax.psum_scatter(grad_right_two.astype(jnp.bfloat16), 'dp', scatter_dimen...  199 us
    unnamed x4, waiting for transfers between devices  149 us
    all_gather x1, blocking collectives, local(): right_two = lax.all_gather(second_right, 'dp', axis=1, tiled=True)  56.4 us
    all_gather x1, blocking collectives, local(): left_two = lax.all_gather(second_left, 'dp', axis=1, tiled=True)  49.4 us
    all_gather x1, blocking collectives, local(): left_one = lax.all_gather(first_left, 'dp', axis=1, tiled=True)  43.4 us
    all_gather x1, blocking collectives, local(): right_one = lax.all_gather(first_right, 'dp', axis=1, tiled=True)  37.2 us
    gather x3, local copies, waits for them, and re-layouts, local(): picked = jnp.take_along_axis(patches, visible[:, :, None], axis=1)  27.8 us
  transfers between devices with their start and end apart: 7, of which 4 were waited for; matrix products, arithmetic and copies ran while one was open for 5% of the time, Pallas kernels for 0%

commit v1 on v0

v1 whole, which is shorter than its diff:
```python
import math

import jax
import jax.numpy as jnp
from jax import lax
from jax.experimental import pallas as pl
from jax.experimental.pallas import tpu as pltpu
from jax.sharding import PartitionSpec as P

BF16 = jnp.bfloat16
F32 = jnp.float32
NB, BS, HB = 64, 96, 256
POS = 6
LB = 4
FEAT = LB * BS
TOK = 2048
TILE = 512
STEPS = TOK // TILE
ROOT_RATIO = math.sqrt(2.0 / math.pi)
DP_ORDER = (8, 4, 2, 1)
PARAMS = pltpu.CompilerParams(vmem_limit_bytes=40 * 1024 * 1024)


def mm(lhs, rhs, left_dim=1, right_dim=0):
    return lax.dot_general(
        lhs, rhs, (((left_dim,), (right_dim,)), ((), ())), preferred_element_type=F32
    )


def whole(shape):
    return pl.BlockSpec(shape, lambda *_: (0,) * len(shape))


def columns(rows):
    return pl.BlockSpec((rows, TILE), lambda step: (0, step))


def token_rows():
    return pl.BlockSpec((TILE, FEAT), lambda step: (step, 0))


def struct(shape, dtype=BF16):
    return jax.ShapeDtypeStruct(shape, dtype)


def cost(flops, moved):
    return pl.CostEstimate(flops=flops, bytes_accessed=moved, transcendentals=0)


def pick_kernel(visible_ref, patches_ref, tokens_ref):
    images, patch_count, _ = patches_ref.shape
    vis = visible_ref.shape[2]
    for image in range(images):
        wanted = visible_ref[image]
        chosen = lax.broadcasted_iota(jnp.int32, (patch_count, vis), 0) == wanted
        rows = mm(chosen.astype(F32).astype(BF16), patches_ref[image], 0, 0)
        tokens_ref[image * vis : (image + 1) * vis, :] = rows.astype(BF16)


def pick(patches, visible):
    images, patch_count, feats = patches.shape
    vis = visible.shape[1]
    group = 8
    return pl.pallas_call(
        pick_kernel,
        grid=(images // group,),
        in_specs=[
            pl.BlockSpec((group, 1, vis), lambda step: (step, 0, 0)),
            pl.BlockSpec((group, patch_count, feats), lambda step: (step, 0, 0)),
        ],
        out_specs=pl.BlockSpec((group * vis, feats), lambda step: (step, 0)),
        out_shape=struct((images * vis, feats)),
        compiler_params=PARAMS,
        cost_estimate=cost(2 * TOK * patch_count * feats, 8 << 20),
        name="pick_patches",
    )(visible[:, None, :], patches)


def up_kernel(tokens_ref, pieces_ref, place_ref, rep_ref, mask_ref, matrix_ref, section_ref):
    @pl.when(pl.program_id(0) == 0)
    def _():
        flat = mm(pieces_ref[...], place_ref[...], 0, 0).astype(BF16)
        matrix_ref[...] = mm(rep_ref[...], flat).astype(BF16) * mask_ref[...]

    section_ref[...] = mm(matrix_ref[...], tokens_ref[...], 1, 1).astype(BF16)


def down_kernel(upstream_ref, pieces_ref, place_ref, tile_ref, mask_ref, matrix_ref, section_ref):
    @pl.when(pl.program_id(0) == 0)
    def _():
        tall = mm(place_ref[...], pieces_ref[...]).astype(BF16)
        matrix_ref[...] = mm(tall, tile_ref[...]).astype(BF16) * mask_ref[...]

    section_ref[...] = mm(matrix_ref[...], upstream_ref[...], 1, 1).astype(BF16)


def block_map(kernel, name, rows, pieces, place, spread, mask):
    return pl.pallas_call(
        kernel,
        grid=(STEPS,),
        in_specs=[
            token_rows(),
            whole(pieces.shape),
            whole(place.shape),
            whole(spread.shape),
            whole(mask.shape),
        ],
        out_specs=[whole((FEAT, FEAT)), columns(FEAT)],
        out_shape=[struct((FEAT, FEAT)), struct((FEAT, TOK))],
        compiler_params=PARAMS,
        cost_estimate=cost(2 * TOK * FEAT * FEAT * 3, 5 << 20),
        name=name,
    )(rows, pieces, place, spread, mask)


def forward_kernel(
    arrived_ref, perm_ref, right_one_ref, right_two_ref, mixed_ref, act_ref, slope_ref, leaving_ref, own_ref
):
    mixed_ref[...] = mm(perm_ref[...], arrived_ref[...]).astype(BF16)
    for pos in range(POS):
        rows = slice(pos * NB, (pos + 1) * NB)
        hidden_rows = slice(pos * HB, (pos + 1) * HB)
        hidden = mm(right_one_ref[pos], mixed_ref[rows, :], 0, 0)
        square = hidden * hidden
        tangent = jnp.tanh(hidden * (ROOT_RATIO + (ROOT_RATIO * 0.044715) * square))
        half = 0.5 * hidden
        act = (half + half * tangent).astype(BF16)
        slope = (0.5 + 0.5 * tangent) + half * (1.0 - tangent * tangent) * (
            ROOT_RATIO + (ROOT_RATIO * 3.0 * 0.044715) * square
        )
        act_ref[hidden_rows, :] = act
        slope_ref[hidden_rows, :] = slope.astype(BF16)
        own_ref[rows, :] = mm(right_two_ref[pos], act, 0, 0).astype(BF16)
    leaving_ref[...] = mm(perm_ref[...], own_ref[...], 0, 0).astype(BF16)


def mix_forward(arrived, perm, right_one, right_two):
    return pl.pallas_call(
        forward_kernel,
        grid=(STEPS,),
        in_specs=[
            columns(FEAT),
            whole((FEAT, FEAT)),
            whole((POS, NB, HB)),
            whole((POS, HB, NB)),
        ],
        out_specs=[columns(FEAT), columns(POS * HB), columns(POS * HB), columns(FEAT)],
        out_shape=[
            struct((FEAT, TOK)),
            struct((POS * HB, TOK)),
            struct((POS * HB, TOK)),
            struct((FEAT, TOK)),
        ],
        scratch_shapes=[pltpu.VMEM((FEAT, TILE), BF16)],
        compiler_params=PARAMS,
        cost_estimate=cost(12 * TOK * FEAT * FEAT, 17 << 20),
        name="mix_forward",
    )(arrived, perm, right_one, right_two)


def backward_kernel(
    arrived_ref,
    perm_ref,
    right_one_ref,
    right_two_ref,
    mixed_ref,
    act_ref,
    slope_ref,
    owner_ref,
    leaving_ref,
    grad_one_ref,
    grad_two_ref,
    grads_ref,
    own_ref,
    sum_one_ref,
    sum_two_ref,
):
    step = pl.program_id(0)

    @pl.when(step == 0)
    def _():
        sum_one_ref[...] = jnp.zeros_like(sum_one_ref)
        sum_two_ref[...] = jnp.zeros_like(sum_two_ref)

    grads_ref[...] = mm(perm_ref[...], arrived_ref[...]).astype(BF16)
    for pos in range(POS):
        rows = slice(pos * NB, (pos + 1) * NB)
        hidden_rows = slice(pos * HB, (pos + 1) * HB)
        grad_act = mm(right_two_ref[pos], grads_ref[rows, :])
        grad_hidden = (grad_act * slope_ref[hidden_rows, :].astype(F32)).astype(BF16)
        own_ref[rows, :] = mm(right_one_ref[pos], grad_hidden).astype(BF16)
        sum_one_ref[rows, :] += mm(mixed_ref[rows, :], grad_hidden, 1, 1)
        sum_two_ref[pos] += mm(act_ref[hidden_rows, :], grads_ref[rows, :], 1, 1)
    leaving_ref[...] = mm(perm_ref[...], own_ref[...], 0, 0).astype(BF16)

    @pl.when(step == STEPS - 1)
    def _():
        grad_one_ref[...] = mm(owner_ref[...], sum_one_ref[...].astype(BF16)).astype(BF16)
        for pos in range(POS // 2):
            pair = jnp.concatenate([sum_two_ref[pos], sum_two_ref[pos + POS // 2]], axis=1)
            pair = pair.astype(BF16)
            for owner in range(16):
                grad_two_ref[owner * 48 + pos * 16 : owner * 48 + pos * 16 + 16, :] = pair[
                    owner * 16 : owner * 16 + 16, :
                ]


def mix_backward(arrived, perm, right_one, right_two, mixed, act, slope, owner):
    return pl.pallas_call(
        backward_kernel,
        grid=(STEPS,),
        in_specs=[
            columns(FEAT),
            whole((FEAT, FEAT)),
            whole((POS, NB, HB)),
            whole((POS, HB, NB)),
            columns(FEAT),
            columns(POS * HB),
            columns(POS * HB),
            whole((FEAT, FEAT)),
        ],
        out_specs=[columns(FEAT), whole((FEAT, HB)), whole((768, 128))],
        out_shape=[struct((FEAT, TOK)), struct((FEAT, HB)), struct((768, 128))],
        scratch_shapes=[
            pltpu.VMEM((FEAT, TILE), BF16),
            pltpu.VMEM((FEAT, TILE), BF16),
            pltpu.VMEM((FEAT, HB), F32),
            pltpu.VMEM((POS, HB, NB), F32),
        ],
        compiler_params=PARAMS,
        cost_estimate=cost(20 * TOK * FEAT * FEAT, 17 << 20),
        name="mix_backward",
    )(arrived, perm, right_one, right_two, mixed, act, slope, owner)


def output_kernel(returned_ref, matrix_ref, upstream_ref, mask_ref, fold_ref, out_ref, grad_ref, sum_ref):
    step = pl.program_id(0)

    @pl.when(step == 0)
    def _():
        sum_ref[...] = jnp.zeros_like(sum_ref)

    out_ref[...] = mm(returned_ref[...], matrix_ref[...], 0, 0).astype(BF16)
    sum_ref[...] += mm(returned_ref[...], upstream_ref[...])

    @pl.when(step == STEPS - 1)
    def _():
        kept = sum_ref[...].astype(BF16) * mask_ref[...]
        grad_ref[...] = mm(kept, fold_ref[...]).astype(BF16)


def output_and_grad(returned, matrix, upstream, mask, fold):
    return pl.pallas_call(
        output_kernel,
        grid=(STEPS,),
        in_specs=[
            columns(FEAT),
            whole((FEAT, FEAT)),
            token_rows(),
            whole((FEAT, FEAT)),
            whole((FEAT, 128)),
        ],
        out_specs=[token_rows(), whole((FEAT, 128))],
        out_shape=[struct((TOK, FEAT)), struct((FEAT, 128))],
        scratch_shapes=[pltpu.VMEM((FEAT, FEAT), F32)],
        compiler_params=PARAMS,
        cost_estimate=cost(4 * TOK * FEAT * FEAT, 5 << 20),
        name="output_and_grad",
    )(returned, matrix, upstream, mask, fold)


def first_grad_kernel(returned_ref, tokens_ref, mask_ref, rep_ref, order_ref, grad_ref, sum_ref):
    step = pl.program_id(0)

    @pl.when(step == 0)
    def _():
        sum_ref[...] = jnp.zeros_like(sum_ref)

    sum_ref[...] += mm(returned_ref[...], tokens_ref[...])

    @pl.when(step == STEPS - 1)
    def _():
        kept = sum_ref[...].astype(BF16) * mask_ref[...]
        flat = mm(rep_ref[...], kept, 0, 0).astype(BF16)
        grad_ref[...] = mm(order_ref[...], flat, 1, 1).astype(BF16)


def first_grad(returned, tokens, mask, rep, order):
    return pl.pallas_call(
        first_grad_kernel,
        grid=(STEPS,),
        in_specs=[
            columns(FEAT),
            token_rows(),
            whole((FEAT, FEAT)),
            whole((FEAT, 128)),
            whole((FEAT, FEAT)),
        ],
        out_specs=whole((FEAT, 128)),
        out_shape=struct((FEAT, 128)),
        scratch_shapes=[pltpu.VMEM((FEAT, FEAT), F32)],
        compiler_params=PARAMS,
        cost_estimate=cost(2 * TOK * FEAT * FEAT, 3 << 20),
        name="first_grad",
    )(returned, tokens, mask, rep, order)


def token_grad_kernel(returned_ref, matrix_ref, out_ref):
    out_ref[...] = mm(returned_ref[...], matrix_ref[...], 0, 0).astype(BF16)


def token_gradient(returned, matrix):
    return pl.pallas_call(
        token_grad_kernel,
        grid=(STEPS,),
        in_specs=[columns(FEAT), whole((FEAT, FEAT))],
        out_specs=token_rows(),
        out_shape=struct((TOK, FEAT)),
        compiler_params=PARAMS,
        cost_estimate=cost(2 * TOK * FEAT * FEAT, 3 << 20),
        name="token_gradient",
    )(returned, matrix)


def gather_pieces(x):
    for bit in DP_ORDER:
        other = lax.ppermute(x, "dp", [(i, i ^ bit) for i in range(16)])
        x = jnp.concatenate([x, other], axis=0)
    return x


def offset(place):
    total = jnp.zeros_like(place)
    for level, bit in enumerate(DP_ORDER):
        total = total + ((place >> level) & 1) * bit
    return total


def to_tensor(x):
    return lax.all_to_all(x, "tensor", split_axis=0, concat_axis=0, tiled=True)


def grid_of(rows, cols):
    return (
        lax.broadcasted_iota(jnp.int32, (rows, cols), 0),
        lax.broadcasted_iota(jnp.int32, (rows, cols), 1),
    )


def local(
    patches, visible, block_perm, first_left, first_right, second_right, second_left, cotangent
):
    me = lax.axis_index("dp").astype(jnp.int32)

    left = gather_pieces(
        jnp.concatenate([first_left.reshape(24, BS), second_left.reshape(24, BS)], axis=0)
    )
    two = second_right.reshape(2, 3, 16, NB).transpose(1, 2, 0, 3).reshape(48, 128)
    one = first_right.reshape(24, HB)
    right = jnp.concatenate([two, one[:, :128], one[:, 128:]], axis=0)

    tokens = pick(patches, visible)

    row, col = grid_of(768, FEAT)
    piece, which, block, rest = row // 48, (row // 24) % 2, (row // 6) % 4, row % 6
    source_row = 6 * (me ^ offset(piece)) + rest
    place_one = ((which == 0) & (block == col // BS) & (source_row == col % BS)).astype(BF16)
    col, row = grid_of(FEAT, 768)
    piece, which, block, rest = row // 48, (row // 24) % 2, (row // 6) % 4, row % 6
    source_row = 6 * (me ^ offset(piece)) + rest
    place_two = ((which == 1) & (block == col % LB) & (source_row == col // LB)).astype(BF16)
    row, col = grid_of(FEAT, FEAT)
    mask = (row % LB == col // BS).astype(BF16)
    order = ((row % LB == col // BS) & (row // LB == col % BS)).astype(BF16)
    owner = (((row // 4) % POS == col // NB) & ((row // 24) * 4 + row % 4 == col % NB)).astype(BF16)
    wanted = jnp.tile(block_perm, POS)[:, None]
    perm = ((row // NB == (col // 4) % POS) & ((col // 24) * 4 + col % 4 == wanted)).astype(BF16)
    row, col = grid_of(FEAT, 128)
    rep = (row // LB == col).astype(BF16)
    fold = (row % BS == col).astype(BF16)
    row, col = grid_of(BS, FEAT)
    spread = (row == col % BS).astype(BF16)

    matrix_one, section_one = block_map(
        up_kernel, "first_map", tokens, left, place_one, rep[:, :BS], mask
    )
    arrived = to_tensor(section_one)
    matrix_two, back_grad = block_map(
        down_kernel, "second_map_back", cotangent, left, place_two, spread, mask
    )
    arrived_grad = to_tensor(back_grad)

    right = gather_pieces(right).reshape(16, 96, 128)
    right = jnp.take(right, offset(jnp.arange(16, dtype=jnp.int32) ^ me), axis=0)
    right_two = (
        right[:, :48].reshape(16, 3, 16, 2, NB).transpose(3, 1, 0, 2, 4).reshape(POS, HB, NB)
    )
    right_one = (
        right[:, 48:].reshape(16, 2, POS, 4, 128).transpose(2, 0, 3, 1, 4).reshape(POS, NB, HB)
    )

    mixed, act, slope, leaving = mix_forward(arrived, perm, right_one, right_two)
    returned = to_tensor(leaving)
    leaving_grad, grad_right_one, grad_right_two = mix_backward(
        arrived_grad, perm, right_one, right_two, mixed, act, slope, owner
    )
    returned_grad = to_tensor(leaving_grad)
    output, grad_left_two = output_and_grad(returned, matrix_two, cotangent, mask, fold)
    grad_left_one = first_grad(returned_grad, tokens, mask, rep, order)
    token_grad = token_gradient(returned_grad, matrix_one)

    shares = jnp.concatenate(
        [
            grad_left_one.reshape(16, 24, 128),
            grad_left_two.reshape(16, 24, 128),
            grad_right_one[:, :128].reshape(16, 24, 128),
            grad_right_one[:, 128:].reshape(16, 24, 128),
            grad_right_two.reshape(16, 48, 128),
        ],
        axis=1,
    )
    shares = lax.all_to_all(shares, "dp", split_axis=0, concat_axis=0, tiled=True)
    total = jnp.sum(shares.astype(F32), axis=0)
    left_total = total[:48, :BS].reshape(2, 6, LB, BS).transpose(0, 2, 1, 3)
    one_total = total[48:96].reshape(2, POS, 4, 128).transpose(1, 2, 0, 3).reshape(POS, 4, HB)
    two_total = total[96:].reshape(3, 16, 2, NB).transpose(2, 0, 1, 3).reshape(POS, 16, NB)
    return (output, token_grad, left_total[0], one_total, two_total, left_total[1])


def solution(mesh):
    placed = (
        P("dp", None, "tensor"),
        P("dp", None),
        P(),
        P("tensor", "dp", None),
        P("tensor", "dp", None),
        P("tensor", "dp", None),
        P("tensor", "dp", None),
        P("dp", "tensor"),
    )
    return jax.shard_map(
        local,
        mesh=mesh,
        in_specs=placed,
        out_specs=(
            P("dp", "tensor"),
            P("dp", "tensor"),
            P("tensor", "dp", None),
            P("tensor", "dp", None),
            P("tensor", "dp", None),
            P("tensor", "dp", None),
        ),
        check_vma=False,
    )
```

time: 900 us -> 252 us (0.28)
  waiting for transfers between devices: 564 us -> 54.2 us
  blocking collectives: 187 us -> 26.3 us
  Pallas kernels: 0 us -> 46.5 us
  matrix products: 36 us -> 0 us
  starting transfers between devices: 22.2 us -> 43.4 us
  between operations: 14.8 us -> 1.3 us
  other arithmetic: 5.61 us -> 18 us
    reduce_scatter x2 -> x0, waiting for transfers between devices: 400 us -> none  [the longest x1 201 us: local(): lax.psum_scatter(grad_right_one.astype(jnp.bfloat16), 'dp', scatter_dimen...]
    all_gather x4 -> x0, blocking collectives: 187 us -> none  [the longest x1 56.4 us: local(): right_two = lax.all_gather(second_right, 'dp', axis=1, tiled=True)]
    unnamed x4 -> x0, waiting for transfers between devices: 149 us -> none
    pallas_call x0 -> x8, Pallas kernels: none -> 46.5 us  [the longest x1 16.5 us: mix_forward(): pl.pallas_call(forward_kernel, grid=(STEPS,), in_specs=[columns(FEAT), wh...]
    dot_general x12 -> x0, matrix products: 36 us -> none  [the longest x1 9.1 us: mix_backward(): jnp.einsum('ptb,pkb->ptk', arrived_grad, down_ordered, preferred_element_...]
    unnamed x55 -> x142, local copies, waits for them, and re-layouts: 9.83 us -> 41.6 us
    gather x7 -> x1, local copies, waits for them, and re-layouts: 31.6 us -> 2.46 us  [local(): jnp.take(right, offset(jnp.arange(16, dtype=jnp.int32) ^ me), axis=0)]
    all_to_all x0 -> x1, blocking collectives: none -> 26.3 us  [to_tensor(): return lax.all_to_all(x, 'tensor', split_axis=0, concat_axis=0, tiled=True)]
  transfers between devices with their start and end apart: 7 -> 12, of which waited for: 4 -> 6; matrix products, arithmetic and copies ran while one was open for 5% -> 16% of each run, Pallas kernels for 0% -> 11%
where the time goes in v1:
time: 252 us; the launch traced here: 250 us
  local copies, waits for them, and re-layouts  60.3 us (24%)
  waiting for transfers between devices  54.2 us (22%)
  Pallas kernels  46.5 us (18%)
  starting transfers between devices  43.4 us (17%)
  blocking collectives  26.3 us (10%)
  other arithmetic  18 us (7%)
    unnamed x142, local copies, waits for them, and re-layouts  41.6 us
    all_to_all x1, blocking collectives, to_tensor(): return lax.all_to_all(x, 'tensor', split_axis=0, concat_axis=0, tiled=True)  26.3 us
    ppermute x8, waiting for transfers between devices, gather_pieces(): other = lax.ppermute(x, 'dp', [(i, i ^ bit) for i in range(16)])  21.6 us
    ppermute x8, starting transfers between devices, gather_pieces(): other = lax.ppermute(x, 'dp', [(i, i ^ bit) for i in range(16)])  18.1 us
    all_to_all x1, waiting for transfers between devices, local(): lax.all_to_all(shares, 'dp', split_axis=0, concat_axis=0, tiled=True)  17.8 us
    all_to_all x3, starting transfers between devices, to_tensor(): return lax.all_to_all(x, 'tensor', split_axis=0, concat_axis=0, tiled=True)  17.1 us
    pallas_call x1, Pallas kernels, mix_forward(): pl.pallas_call(forward_kernel, grid=(STEPS,), in_specs=[columns(FEAT), wh...  16.5 us
    all_to_all x3, waiting for transfers between devices, to_tensor(): return lax.all_to_all(x, 'tensor', split_axis=0, concat_axis=0, tiled=True)  14.9 us
  transfers between devices with their start and end apart: 12, of which 6 were waited for; matrix products, arithmetic and copies ran while one was open for 16% of the time, Pallas kernels for 11%

profile of v1, /device:TPU:2, one launch (start us, length us, event | category | flops | bytes accessed | tf_op | source)
XLA Modules:
  0.0 249.9 jit_solution(4360399094075320182)
XLA Ops:
  2.1 7.3 %collective-permute-start = (bf16[48,96]{1,0:T(8,128)(2,1)S(1)}, bf16[48,96]{1,0:T(8,128)(2,1)S(1)}, u32[]{:S(2)}, u32[]{:S(2)}) collective-permute-start(bf16[48,96]{1,0:T(8,128)(2,1)S(1)} %pad_maximum_fusion.4), channel_id=1, source_target_pairs={{0,128},{16,144},{32,160},{48,176},{64,192},{80,208},{96,224},{112... | collective-permute-start | bytes 27656 | tf_op jit(solution)/shard_map/ppermute | solution.py:327
  15.9 1.2 fusion.56
  17.1 1.6 fusion.38.place_ref
  19.4 2.1 collective-permute-start.1
  21.6 2.7 %collective-permute-done.1 = bf16[96,96]{1,0:T(8,128)(2,1)S(1)} collective-permute-done((bf16[96,96]{1,0:T(8,128)(2,1)S(1)}, bf16[96,96]{1,0:T(8,128)(2,1)S(1)}, u32[]{:S(2)}, u32[]{:S(2)}) %collective-permute-start.1) | collective-permute-done | bytes 18464 | tf_op jit(solution)/shard_map/ppermute | solution.py:327
  25.4 3.1 %collective-permute-done.2 = bf16[192,96]{1,0:T(8,128)(2,1)S(1)} collective-permute-done((bf16[192,96]{1,0:T(8,128)(2,1)S(1)}, bf16[192,96]{1,0:T(8,128)(2,1)S(1)}, u32[]{:S(2)}, u32[]{:S(2)}) %collective-permute-start.2) | collective-permute-done | bytes 36896 | tf_op jit(solution)/shard_map/ppermute | solution.py:327
  28.5 2.2 collective-permute-start.3
  31.3 2.8 %copy-done = bf16[32,256,384]{2,1,0:T(8,128)(2,1)S(1)} copy-done((bf16[32,256,384]{2,1,0:T(8,128)(2,1)S(1)}, bf16[32,256,384]{2,1,0:T(8,128)(2,1)}, u32[]{:S(2)}) %copy-start) | copy-done | bytes 6291480
  34.1 1.6 pick_patches.1.tokens_ref
  35.8 2.2 first_map.1
  39.9 5.9 %all-to-all-start = ((bf16[16,24,2048]{2,1,0:T(8,128)(2,1)}), bf16[16,24,2048]{2,1,0:T(8,128)(2,1)S(1)}, u32[]{:S(2)}, u32[]{:S(2)}) async-start(bf16[16,24,2048]{2,1,0:T(8,128)(2,1)} %bitcast.45), calls=%async_computation | async-start | bytes 3145728 | tf_op jit(solution)/shard_map/all_to_all | solution.py:340
  45.8 1.3 constant_dynamic-update-slice_fusion.13
  47.1 1.3 fusion.60.tile_ref
  48.4 2.6 %fusion.39.place_ref = bf16[384,768]{1,0:T(8,128)(2,1)} fusion(s32[384]{0:T(512)S(1)} %get-tuple-element.90, s32[384]{0:T(512)} %copy-done.34, s32[768]{0:T(1024)} %copy-done.47, s32[768]{0:T(1024)} %copy-done.48, s32[768]{0:T(1024)} %copy-done.51, s32[768]{0:T(1024)} %copy-done.49, s32[]{:T(128)S(6)} %axis_index.15, s32[384]{0:T(512)} %copy-done.38, ...), kind=kLoop, calls=%fused_computation.69 | loop fusion | flops 15040512 | bytes 624388 | tf_op jit(solution)/shard_map/convert_element_type | solution.py:371
  51.5 1.2 tile.2
  52.8 1.4 eq.92
  54.2 1.4 pad_maximum_fusion.1
  55.5 2.0 collective-permute-start.5
  57.5 1.4 constant_dynamic-update-slice_fusion.18
  61.7 1.4 copy-done.23
  63.2 2.3 second_map_back.1
  67.4 5.7 %all-to-all-start.2 = ((bf16[16,24,2048]{2,1,0:T(8,128)(2,1)}), bf16[16,24,2048]{2,1,0:T(8,128)(2,1)}, u32[]{:S(2)}, u32[]{:S(2)}) async-start(bf16[16,24,2048]{2,1,0:T(8,128)(2,1)} %bitcast.44), calls=%async_computation.2 | async-start | bytes 3145728 | tf_op jit(solution)/shard_map/all_to_all | solution.py:340
  73.1 1.5 constant_dynamic-update-slice_fusion.17
  74.6 1.9 collective-permute-start.6
  77.0 2.8 %collective-permute-done.6 = bf16[384,128]{1,0:T(8,128)(2,1)S(1)} collective-permute-done((bf16[384,128]{1,0:T(8,128)(2,1)}, bf16[384,128]{1,0:T(8,128)(2,1)S(1)}, u32[]{:S(2)}, u32[]{:S(2)}) %collective-permute-start.6) | collective-permute-done | bytes 98336 | tf_op jit(solution)/shard_map/ppermute | solution.py:327
  80.5 1.4 collective-permute-start.7
  82.0 2.8 %fusion.51 = (bf16[384,384]{1,0:T(8,128)(2,1)}, bf16[384,384]{1,0:T(8,128)(2,1)}) fusion(s32[384]{0:T(512)} %get-tuple-element.98, s32[384]{0:T(512)} %get-tuple-element.99, s32[384]{0:T(512)} %get-tuple-element.96, s32[384]{0:T(512)} %get-tuple-element.102, s32[384]{0:T(512)} %get-tuple-element.97, s32[384]{0:T(512)} %get-tuple-element.103, ...), kind=kLoop, calls=%fused_computation.89 | loop fusion | flops 4866048 | bytes 608640 | tf_op jit(solution)/shard_map/convert_element_type | solution.py:375
  84.8 13.0 %collective-permute-done.7 = bf16[768,128]{1,0:T(8,128)(2,1)S(1)} collective-permute-done((bf16[768,128]{1,0:T(8,128)(2,1)}, bf16[768,128]{1,0:T(8,128)(2,1)S(1)}, u32[]{:S(2)}, u32[]{:S(2)}) %collective-permute-start.7) | collective-permute-done | bytes 196640 | tf_op jit(solution)/shard_map/ppermute | solution.py:327
  98.5 2.5 gather_fusion
  103.8 1.7 reshape.152.right_one_ref
  105.5 1.9 reshape.153
  110.3 16.5 %mix_forward.1 = (bf16[384,2048]{1,0:T(8,128)(2,1)S(1)}, bf16[1536,2048]{1,0:T(8,128)(2,1)S(1)}, bf16[1536,2048]{1,0:T(8,128)(2,1)}, bf16[384,2048]{1,0:T(8,128)(2,1)S(1)}) custom-call(bf16[384,2048]{1,0:T(8,128)(2,1)S(1)} %bitcast.43, bf16[384,384]{1,0:T(8,128)(2,1)S(1)} %copy-done.9, bf16[6,64,256]{2,1,0:T(8,128)(2,1)S(1)} %copy-done.15, ...), custom_call_target="tpu_custom_call" | custom-call | flops 3623878656 | bytes 17825792 | tf_op jit(solution)/shard_map/mix_forward/pallas_call | solution.py:138
  126.8 1.1 copy-done.3
  128.6 2.7 %copy-done.27 = bf16[1536,2048]{1,0:T(8,128)(2,1)} copy-done((bf16[1536,2048]{1,0:T(8,128)(2,1)}, bf16[1536,2048]{1,0:T(8,128)(2,1)S(1)}, u32[]{:S(2)}) %copy-start.27) | copy-done | bytes 6291480
  131.4 1.1 copy-done.29
  136.4 2.8 %copy-done.28 = bf16[1536,2048]{1,0:T(8,128)(2,1)S(1)} copy-done((bf16[1536,2048]{1,0:T(8,128)(2,1)S(1)}, bf16[1536,2048]{1,0:T(8,128)(2,1)}, u32[]{:S(2)}) %copy-start.28) | copy-done | bytes 6291480
  139.1 1.4 copy-done.30
  140.5 13.5 %mix_backward.1 = (bf16[384,2048]{1,0:T(8,128)(2,1)S(1)}, bf16[384,256]{1,0:T(8,128)(2,1)S(1)}, bf16[768,128]{1,0:T(8,128)(2,1)S(1)}) custom-call(bf16[384,2048]{1,0:T(8,128)(2,1)} %bitcast.14.arrived_ref, bf16[384,384]{1,0:T(8,128)(2,1)S(1)} %copy-done.10, bf16[6,64,256]{2,1,0:T(8,128)(2,1)S(1)} %copy-done.16, bf16[6,256,64]{2,1,0:T(8,128)(2,1)S(1)} %bitcast.49, ...), custom_call_target="tpu_custom_call" | custom-call | flops 6039797760 | bytes 17825792 | tf_op jit(solution)/shard_map/mix_backward/pallas_call | solution.py:209
  154.7 26.3 %all_to_all.49 = bf16[16,24,2048]{2,1,0:T(8,128)(2,1)S(1)} all-to-all(bf16[16,24,2048]{2,1,0:T(8,128)(2,1)S(1)} %bitcast.47), channel_id=1, replica_groups=mesh['dp'=16,'tensor'=16] {'tensor'}, dimensions={0} | all-to-all | bytes 3145728 | tf_op jit(solution)/shard_map/all_to_all | solution.py:340
  181.0 5.4 %all-to-all-start.1 = ((bf16[16,24,2048]{2,1,0:T(8,128)(2,1)}), bf16[16,24,2048]{2,1,0:T(8,128)(2,1)}, u32[]{:S(2)}, u32[]{:S(2)}) async-start(bf16[16,24,2048]{2,1,0:T(8,128)(2,1)} %bitcast.46), calls=%async_computation.1 | async-start | bytes 3145728 | tf_op jit(solution)/shard_map/all_to_all | solution.py:340
  187.2 1.6 fusion.91
  189.8 2.2 first_grad.1
  192.7 14.9 %all-to-all-done.1 = bf16[16,24,2048]{2,1,0:T(8,128)(2,1)} async-done(((bf16[16,24,2048]{2,1,0:T(8,128)(2,1)}), bf16[16,24,2048]{2,1,0:T(8,128)(2,1)}, u32[]{:S(2)}, u32[]{:S(2)}) %all-to-all-start.1) | async-done | bytes 1572896 | tf_op jit(solution)/shard_map/all_to_all | solution.py:340
  208.4 1.4 copy-done.24
  210.8 5.2 %output_and_grad.1 = (bf16[2048,384]{1,0:T(8,128)(2,1)}, bf16[384,128]{1,0:T(8,128)(2,1)S(1)}) custom-call(bf16[384,2048]{1,0:T(8,128)(2,1)} %bitcast.12.returned_ref, bf16[384,384]{1,0:T(8,128)(2,1)S(1)} %copy-done.26, bf16[2048,384]{1,0:T(8,128)(2,1)S(1)} %copy-done.24, bf16[384,384]{1,0:T(8,128)(2,1)S(1)} %get-tuple-element.67.mask_ref, ...), custom_call_target="tpu_custom_call" | custom-call | flops 1207959552 | bytes 5242880 | tf_op jit(solution)/shard_map/output_and_grad/pallas_call | solution.py:253
  218.8 8.3 %all-to-all-start.4 = ((bf16[16,144,128]{2,1,0:T(8,128)(2,1)}), bf16[16,144,128]{2,1,0:T(8,128)(2,1)S(1)}, u32[]{:S(2)}, u32[]{:S(2)}) async-start(bf16[16,144,128]{2,1,0:T(8,128)(2,1)} %constant_dynamic-update-slice_fusion.29), calls=%async_computation.4 | async-start | bytes 1179648 | tf_op jit(solution)/shard_map/all_to_all | solution.py:422
  227.1 3.0 %token_gradient.1 = bf16[2048,384]{1,0:T(8,128)(2,1)} custom-call(bf16[384,2048]{1,0:T(8,128)(2,1)S(1)} %bitcast.42, bf16[384,384]{1,0:T(8,128)(2,1)S(1)} %copy-done.12), custom_call_target="tpu_custom_call" | custom-call | flops 603979776 | bytes 3145728 | tf_op jit(solution)/shard_map/token_gradient/pallas_call | solution.py:313
  230.1 17.8 %all-to-all-done.4 = bf16[16,144,128]{2,1,0:T(8,128)(2,1)S(1)} async-done(((bf16[16,144,128]{2,1,0:T(8,128)(2,1)}), bf16[16,144,128]{2,1,0:T(8,128)(2,1)S(1)}, u32[]{:S(2)}, u32[]{:S(2)}) %all-to-all-start.4) | async-done | bytes 589856 | tf_op jit(solution)/shard_map/all_to_all | solution.py:422
  (188 shorter events, 39.3 us)
Async XLA Ops:
  0.6 30.7 %copy-start.20 = (s32[32,64]{1,0:T(8,128)S(1)}, s32[32,64]{1,0:T(8,128)}, u32[]{:S(2)}) copy-start(s32[32,64]{1,0:T(8,128)} %param.9) | copy-start | bytes 24580
  2.1 17.3 %collective-permute-start = (bf16[48,96]{1,0:T(8,128)(2,1)S(1)}, bf16[48,96]{1,0:T(8,128)(2,1)S(1)}, u32[]{:S(2)}, u32[]{:S(2)}) collective-permute-start(bf16[48,96]{1,0:T(8,128)(2,1)S(1)} %pad_maximum_fusion.4), channel_id=1, source_target_pairs={{0,128},{16,144},{32,160},{48,176},{64,192},{80,208},{96,224},{112... | collective-permute-start | bytes 27656 | tf_op jit(solution)/shard_map/ppermute | solution.py:327
  13.4 40.7 %collective-permute-start.4 = (bf16[96,128]{1,0:T(8,128)(2,1)}, bf16[96,128]{1,0:T(8,128)(2,1)}, u32[]{:S(2)}, u32[]{:S(2)}) collective-permute-start(bf16[96,128]{1,0:T(8,128)(2,1)} %pad_maximum_fusion.3), channel_id=1, source_target_pairs={{0,128},{16,144},{32,160},{48,176},{64,192},{80,208},{96,224},{112... | collective-permute-start | bytes 73736 | tf_op jit(solution)/shard_map/ppermute | solution.py:327
  13.5 5.8 %copy-start.42 = (s32[384]{0:T(512)}, s32[384]{0:T(512)S(1)}, u32[]{:S(2)}) copy-start(s32[384]{0:T(512)S(1)} %get-tuple-element.83) | copy-start | bytes 4612
  13.6 5.8 %copy-start.44 = (s32[384]{0:T(512)}, s32[384]{0:T(512)S(1)}, u32[]{:S(2)}) copy-start(s32[384]{0:T(512)S(1)} %get-tuple-element.84) | copy-start | bytes 4612
  13.6 5.8 %copy-start.46 = (s32[768]{0:T(1024)}, s32[768]{0:T(1024)S(1)}, u32[]{:S(2)}) copy-start(s32[768]{0:T(1024)S(1)} %get-tuple-element.72) | copy-start | bytes 9220
  13.6 7.9 %copy-start.47 = (s32[768]{0:T(1024)}, s32[768]{0:T(1024)S(1)}, u32[]{:S(2)}) copy-start(s32[768]{0:T(1024)S(1)} %get-tuple-element.73) | copy-start | bytes 9220
  13.6 7.9 %copy-start.48 = (s32[768]{0:T(1024)}, s32[768]{0:T(1024)S(1)}, u32[]{:S(2)}) copy-start(s32[768]{0:T(1024)S(1)} %get-tuple-element.76) | copy-start | bytes 9220
  13.6 7.9 %copy-start.49 = (s32[768]{0:T(1024)}, s32[768]{0:T(1024)S(1)}, u32[]{:S(2)}) copy-start(s32[768]{0:T(1024)S(1)} %get-tuple-element.77) | copy-start | bytes 9220
  13.6 7.9 %copy-start.50 = (s32[768]{0:T(1024)}, s32[768]{0:T(1024)S(1)}, u32[]{:S(2)}) copy-start(s32[768]{0:T(1024)S(1)} %get-tuple-element.74) | copy-start | bytes 9220
  13.7 7.9 %copy-start.51 = (s32[768]{0:T(1024)}, s32[768]{0:T(1024)S(1)}, u32[]{:S(2)}) copy-start(s32[768]{0:T(1024)S(1)} %get-tuple-element.75) | copy-start | bytes 9220
  13.7 7.9 %copy-start.52 = (s32[768]{0:T(1024)}, s32[768]{0:T(1024)S(1)}, u32[]{:S(2)}) copy-start(s32[768]{0:T(1024)S(1)} %get-tuple-element.86) | copy-start | bytes 9220
  13.7 7.9 %copy-start.53 = (s32[768]{0:T(1024)}, s32[768]{0:T(1024)S(1)}, u32[]{:S(2)}) copy-start(s32[768]{0:T(1024)S(1)} %get-tuple-element.87) | copy-start | bytes 9220
  13.7 10.5 %copy-start.55 = (pred[768]{0:T(1024)(128)(4,1)}, pred[768]{0:T(1024)(128)(4,1)S(1)}, u32[]{:S(2)}) copy-start(pred[768]{0:T(1024)(128)(4,1)S(1)} %get-tuple-element.78) | copy-start | bytes 2308
  13.7 10.5 %copy-start.56 = (pred[768]{0:T(1024)(128)(4,1)}, pred[768]{0:T(1024)(128)(4,1)S(1)}, u32[]{:S(2)}) copy-start(pred[768]{0:T(1024)(128)(4,1)S(1)} %get-tuple-element.79) | copy-start | bytes 2308
  13.8 10.5 %copy-start.57 = (pred[768]{0:T(1024)(128)(4,1)}, pred[768]{0:T(1024)(128)(4,1)S(1)}, u32[]{:S(2)}) copy-start(pred[768]{0:T(1024)(128)(4,1)S(1)} %get-tuple-element.80) | copy-start | bytes 2308
  13.8 10.5 %copy-start.58 = (pred[768]{0:T(1024)(128)(4,1)}, pred[768]{0:T(1024)(128)(4,1)S(1)}, u32[]{:S(2)}) copy-start(pred[768]{0:T(1024)(128)(4,1)S(1)} %get-tuple-element.81) | copy-start | bytes 2308
  13.8 10.5 %copy-start.59 = (pred[384]{0:T(512)(128)(4,1)}, pred[384]{0:T(512)(128)(4,1)S(1)}, u32[]{:S(2)}) copy-start(pred[384]{0:T(512)(128)(4,1)S(1)} %get-tuple-element.88) | copy-start | bytes 1156
  13.8 5.6 %copy-start.34 = (s32[384]{0:T(512)}, s32[384]{0:T(512)S(1)}, u32[]{:S(2)}) copy-start(s32[384]{0:T(512)S(1)} %get-tuple-element.91) | copy-start | bytes 4612
  13.8 5.5 %copy-start.54 = (pred[384]{0:T(512)(128)(4,1)}, pred[384]{0:T(512)(128)(4,1)S(1)}, u32[]{:S(2)}) copy-start(pred[384]{0:T(512)(128)(4,1)S(1)} %get-tuple-element.95) | copy-start | bytes 1156
  13.8 10.4 %copy-start.61 = (pred[384]{0:T(512)(128)(4,1)}, pred[384]{0:T(512)(128)(4,1)S(1)}, u32[]{:S(2)}) copy-start(pred[384]{0:T(512)(128)(4,1)S(1)} %get-tuple-element.94) | copy-start | bytes 1156
  13.9 5.5 %copy-start.38 = (s32[384]{0:T(512)}, s32[384]{0:T(512)S(1)}, u32[]{:S(2)}) copy-start(s32[384]{0:T(512)S(1)} %get-tuple-element.92) | copy-start | bytes 4612
  13.9 5.5 %copy-start.40 = (s32[384]{0:T(512)}, s32[384]{0:T(512)S(1)}, u32[]{:S(2)}) copy-start(s32[384]{0:T(512)S(1)} %get-tuple-element.93) | copy-start | bytes 4612
  19.4 4.8 %collective-permute-start.1 = (bf16[96,96]{1,0:T(8,128)(2,1)S(1)}, bf16[96,96]{1,0:T(8,128)(2,1)S(1)}, u32[]{:S(2)}, u32[]{:S(2)}) collective-permute-start(bf16[96,96]{1,0:T(8,128)(2,1)S(1)} %pad_maximum_fusion.2), channel_id=1, source_target_pairs={{0,64},{16,80},{32,96},{48,112},{64,0},{80,16},{96,32},{112,48},{1... | collective-permute-start | bytes 55304 | tf_op jit(solution)/shard_map/ppermute | solution.py:327
  24.3 4.2 %collective-permute-start.2 = (bf16[192,96]{1,0:T(8,128)(2,1)S(1)}, bf16[192,96]{1,0:T(8,128)(2,1)S(1)}, u32[]{:S(2)}, u32[]{:S(2)}) collective-permute-start(bf16[192,96]{1,0:T(8,128)(2,1)S(1)} %pad_maximum_fusion), channel_id=1, source_target_pairs={{0,32},{16,48},{32,0},{48,16},{64,96},{80,112},{96,64},{112,80},{1... | collective-permute-start | bytes 110600 | tf_op jit(solution)/shard_map/ppermute | solution.py:327
  28.5 7.2 %collective-permute-start.3 = (bf16[384,96]{1,0:T(8,128)(2,1)S(1)}, bf16[384,96]{1,0:T(8,128)(2,1)S(1)}, u32[]{:S(2)}, u32[]{:S(2)}) collective-permute-start(bf16[384,96]{1,0:T(8,128)(2,1)S(1)} %get-tuple-element.43), channel_id=1, source_target_pairs={{0,16},{16,0},{32,48},{48,32},{64,80},{80,64},{96,112},{112,96},{1... | collective-permute-start | bytes 221192 | tf_op jit(solution)/shard_map/ppermute | solution.py:327
  31.3 2.8 %copy-start = (bf16[32,256,384]{2,1,0:T(8,128)(2,1)S(1)}, bf16[32,256,384]{2,1,0:T(8,128)(2,1)}, u32[]{:S(2)}) copy-start(bf16[32,256,384]{2,1,0:T(8,128)(2,1)} %patches_ref.1) | copy-start | bytes 18874372
  39.9 27.5 %all-to-all-start = ((bf16[16,24,2048]{2,1,0:T(8,128)(2,1)}), bf16[16,24,2048]{2,1,0:T(8,128)(2,1)S(1)}, u32[]{:S(2)}, u32[]{:S(2)}) async-start(bf16[16,24,2048]{2,1,0:T(8,128)(2,1)} %bitcast.45), calls=%async_computation | async-start | bytes 3145728 | tf_op jit(solution)/shard_map/all_to_all | solution.py:340
  55.5 17.6 %collective-permute-start.5 = (bf16[192,128]{1,0:T(8,128)(2,1)}, bf16[192,128]{1,0:T(8,128)(2,1)}, u32[]{:S(2)}, u32[]{:S(2)}) collective-permute-start(bf16[192,128]{1,0:T(8,128)(2,1)} %pad_maximum_fusion.1), channel_id=1, source_target_pairs={{0,64},{16,80},{32,96},{48,112},{64,0},{80,16},{96,32},{112,48},{1... | collective-permute-start | bytes 147464 | tf_op jit(solution)/shard_map/ppermute | solution.py:327
  67.4 14.6 %copy-start.35 = (s32[384]{0:T(512)S(1)}, s32[384]{0:T(512)}, u32[]{:S(2)}) copy-start(s32[384]{0:T(512)} %copy-done.34) | copy-start | bytes 4612
  67.4 14.6 %copy-start.39 = (s32[384]{0:T(512)S(1)}, s32[384]{0:T(512)}, u32[]{:S(2)}) copy-start(s32[384]{0:T(512)} %copy-done.38) | copy-start | bytes 4612
  67.4 14.6 %copy-start.41 = (s32[384]{0:T(512)S(1)}, s32[384]{0:T(512)}, u32[]{:S(2)}) copy-start(s32[384]{0:T(512)} %copy-done.40) | copy-start | bytes 4612
  67.4 65.1 %all-to-all-start.2 = ((bf16[16,24,2048]{2,1,0:T(8,128)(2,1)}), bf16[16,24,2048]{2,1,0:T(8,128)(2,1)}, u32[]{:S(2)}, u32[]{:S(2)}) async-start(bf16[16,24,2048]{2,1,0:T(8,128)(2,1)} %bitcast.44), calls=%async_computation.2 | async-start | bytes 3145728 | tf_op jit(solution)/shard_map/all_to_all | solution.py:340
  74.6 5.2 %collective-permute-start.6 = (bf16[384,128]{1,0:T(8,128)(2,1)}, bf16[384,128]{1,0:T(8,128)(2,1)S(1)}, u32[]{:S(2)}, u32[]{:S(2)}) collective-permute-start(bf16[384,128]{1,0:T(8,128)(2,1)} %get-tuple-element.42), channel_id=1, source_target_pairs={{0,32},{16,48},{32,0},{48,16},{64,96},{80,112},{96,64},{112,80},{1... | collective-permute-start | bytes 294920 | tf_op jit(solution)/shard_map/ppermute | solution.py:327
  80.5 17.3 %collective-permute-start.7 = (bf16[768,128]{1,0:T(8,128)(2,1)}, bf16[768,128]{1,0:T(8,128)(2,1)S(1)}, u32[]{:S(2)}, u32[]{:S(2)}) collective-permute-start(bf16[768,128]{1,0:T(8,128)(2,1)} %get-tuple-element.36), channel_id=1, source_target_pairs={{0,16},{16,0},{32,48},{48,32},{64,80},{80,64},{96,112},{112,96},{1... | collective-permute-start | bytes 589832 | tf_op jit(solution)/shard_map/ppermute | solution.py:327
  84.8 16.2 %copy-start.62 = (pred[16]{0:T(512)(128)(4,1)S(1)}, pred[16]{0:T(512)(128)(4,1)}, u32[]{:S(2)}) copy-start(pred[16]{0:T(512)(128)(4,1)} %compare_and_fusion) | copy-start | bytes 52
  128.6 2.7 %copy-start.27 = (bf16[1536,2048]{1,0:T(8,128)(2,1)}, bf16[1536,2048]{1,0:T(8,128)(2,1)S(1)}, u32[]{:S(2)}) copy-start(bf16[1536,2048]{1,0:T(8,128)(2,1)S(1)} %get-tuple-element.25.act_ref) | copy-start | bytes 18874372
  136.4 2.8 %copy-start.28 = (bf16[1536,2048]{1,0:T(8,128)(2,1)S(1)}, bf16[1536,2048]{1,0:T(8,128)(2,1)}, u32[]{:S(2)}) copy-start(bf16[1536,2048]{1,0:T(8,128)(2,1)} %copy-done.27) | copy-start | bytes 18874372
  154.7 26.3 %copy-start.17 = (bf16[384,256]{1,0:T(8,128)(2,1)}, bf16[384,256]{1,0:T(8,128)(2,1)S(1)}, u32[]{:S(2)}) copy-start(bf16[384,256]{1,0:T(8,128)(2,1)S(1)} %get-tuple-element.30) | copy-start | bytes 589828
  181.0 5.4 %copy-start.43 = (s32[384]{0:T(512)S(1)}, s32[384]{0:T(512)}, u32[]{:S(2)}) copy-start(s32[384]{0:T(512)} %copy-done.42) | copy-start | bytes 4612
  181.0 5.4 %copy-start.45 = (s32[384]{0:T(512)S(1)}, s32[384]{0:T(512)}, u32[]{:S(2)}) copy-start(s32[384]{0:T(512)} %copy-done.44) | copy-start | bytes 4612
  181.0 5.4 %copy-start.60 = (pred[384]{0:T(512)(128)(4,1)S(1)}, pred[384]{0:T(512)(128)(4,1)}, u32[]{:S(2)}) copy-start(pred[384]{0:T(512)(128)(4,1)} %copy-done.59) | copy-start | bytes 1156
  181.0 26.5 %all-to-all-start.1 = ((bf16[16,24,2048]{2,1,0:T(8,128)(2,1)}), bf16[16,24,2048]{2,1,0:T(8,128)(2,1)}, u32[]{:S(2)}, u32[]{:S(2)}) async-start(bf16[16,24,2048]{2,1,0:T(8,128)(2,1)} %bitcast.46), calls=%async_computation.1 | async-start | bytes 3145728 | tf_op jit(solution)/shard_map/all_to_all | solution.py:340
  210.8 5.9 %copy-start.32 = (bf16[384,128]{1,0:T(8,128)(2,1)S(1)}, bf16[384,128]{1,0:T(8,128)(2,1)}, u32[]{:S(2)}) copy-start(bf16[384,128]{1,0:T(8,128)(2,1)} %get-tuple-element.35) | copy-start | bytes 294916
  210.8 6.6 %copy-start.31 = (bf16[384,128]{1,0:T(8,128)(2,1)S(1)}, bf16[384,128]{1,0:T(8,128)(2,1)}, u32[]{:S(2)}) copy-start(bf16[384,128]{1,0:T(8,128)(2,1)} %get-tuple-element.34) | copy-start | bytes 294916
  210.8 7.3 %copy-start.14 = (bf16[768,128]{1,0:T(8,128)(2,1)S(1)}, bf16[768,128]{1,0:T(8,128)(2,1)}, u32[]{:S(2)}) copy-start(bf16[768,128]{1,0:T(8,128)(2,1)} %copy-done.13) | copy-start | bytes 589828
  216.0 11.1 %copy-start.12 = (bf16[384,384]{1,0:T(8,128)(2,1)S(1)}, bf16[384,384]{1,0:T(8,128)(2,1)}, u32[]{:S(2)}) copy-start(bf16[384,384]{1,0:T(8,128)(2,1)} %copy-done.11) | copy-start | bytes 884740
  218.8 29.1 %all-to-all-start.4 = ((bf16[16,144,128]{2,1,0:T(8,128)(2,1)}), bf16[16,144,128]{2,1,0:T(8,128)(2,1)S(1)}, u32[]{:S(2)}, u32[]{:S(2)}) async-start(bf16[16,144,128]{2,1,0:T(8,128)(2,1)} %constant_dynamic-update-slice_fusion.29), calls=%async_computation.4 | async-start | bytes 1179648 | tf_op jit(solution)/shard_map/all_to_all | solution.py:422
  (27 other events, 28.4 us)

commit v2 on v1

v2 whole, which is shorter than its diff:
```python
import math

import jax
import jax.numpy as jnp
from jax import lax
from jax.experimental import pallas as pl
from jax.experimental.pallas import tpu as pltpu
from jax.sharding import PartitionSpec as P

BF16 = jnp.bfloat16
F32 = jnp.float32
NB, BS, HB = 64, 96, 256
POS = 6
LB = 4
FEAT = LB * BS
TOK = 2048
PIECES = 16
ALL_ROWS = 768
TILE = 512
STEPS = TOK // TILE
WIDE = 1024
WIDE_STEPS = TOK // WIDE
ROOT_RATIO = math.sqrt(2.0 / math.pi)
DP_ORDER = (1, 8, 4, 2)
PARAMS = pltpu.CompilerParams(vmem_limit_bytes=63 * 1024 * 1024)


def mm(lhs, rhs, left_dim=1, right_dim=0):
    return lax.dot_general(
        lhs, rhs, (((left_dim,), (right_dim,)), ((), ())), preferred_element_type=F32
    )


def whole(shape):
    return pl.BlockSpec(shape, lambda *_: (0,) * len(shape))


def columns(rows, tile=TILE):
    return pl.BlockSpec((rows, tile), lambda step: (0, step))


def token_rows():
    return pl.BlockSpec((WIDE, FEAT), lambda step: (step, 0))


def piece_rows(part):
    return pl.BlockSpec((PIECES, 48, 128), lambda *_: (0, part, 0))


def struct(shape, dtype=BF16):
    return jax.ShapeDtypeStruct(shape, dtype)


def cost(flops, moved):
    return pl.CostEstimate(flops=flops, bytes_accessed=moved, transcendentals=0)


def offset(place):
    return sum(((place >> level) & 1) * bit for level, bit in enumerate(DP_ORDER))


def prepare_kernel(
    perm_ref,
    visible_ref,
    patches_ref,
    tokens_ref,
    place_one_ref,
    place_two_ref,
    owner_ref,
    mix_ref,
    mask_ref,
    rep_ref,
    fold_ref,
    spread_ref,
):
    images, patch_count, _ = patches_ref.shape
    vis = visible_ref.shape[2]
    for image in range(images):
        wanted = visible_ref[image]
        chosen = lax.broadcasted_iota(jnp.int32, (patch_count, vis), 0) == wanted
        rows = mm(chosen.astype(F32).astype(BF16), patches_ref[image], 0, 0)
        tokens_ref[image * vis : (image + 1) * vis, :] = rows.astype(BF16)

    @pl.when(pl.program_id(0) == 0)
    def _():
        def tall(rows):
            return lax.broadcasted_iota(jnp.int32, (rows, 1), 0)

        def wide(cols):
            return lax.broadcasted_iota(jnp.int32, (1, cols), 1)

        def equal(left, right):
            return (left == right).astype(F32).astype(BF16)

        def parts(row, inner):
            outer = lax.div(row, inner)
            return outer, row - outer * inner

        def left_keys(row):
            piece, rest = parts(row, 48)
            which, rest = parts(rest, 24)
            near, block = parts(rest, LB)
            return which, piece * 6 + near, block

        which, source, block = left_keys(tall(ALL_ROWS))
        place_one_ref[...] = equal(jnp.where(which == 0, block * BS + source, -1), wide(FEAT))
        place_two_ref[...] = equal(jnp.where(which == 1, source * LB + block, -1), wide(FEAT))

        piece, rest = parts(tall(ALL_ROWS), 48)
        half, rest = parts(rest, 24)
        pos, near = parts(rest, 4)
        key = half * FEAT + pos * NB + piece * 4 + near
        owner_ref[...] = equal(key, wide(ALL_ROWS))

        piece, rest = parts(tall(FEAT), 24)
        pos, near = parts(rest, 4)
        blocks = jnp.concatenate([perm_ref[...]] * POS, axis=1)
        at, _ = parts(wide(FEAT), NB)
        mix_ref[...] = equal(pos * NB + piece * 4 + near, at * NB + blocks)

        outer, inner = parts(tall(FEAT), LB)
        block, within = parts(wide(FEAT), BS)
        mask_ref[...] = equal(inner, block)
        rep_ref[...] = equal(outer, wide(128))
        _, row_within = parts(tall(FEAT), BS)
        fold_ref[...] = equal(row_within, wide(128))
        spread_ref[...] = equal(tall(128), within)


def prepare(block_perm, visible, patches):
    images, patch_count, feats = patches.shape
    vis = visible.shape[1]
    group = 8
    shapes = [
        (ALL_ROWS, FEAT),
        (ALL_ROWS, FEAT),
        (ALL_ROWS, ALL_ROWS),
        (FEAT, FEAT),
        (FEAT, FEAT),
        (FEAT, 128),
        (FEAT, 128),
        (128, FEAT),
    ]
    return pl.pallas_call(
        prepare_kernel,
        grid=(images // group,),
        in_specs=[
            whole((1, NB)),
            pl.BlockSpec((group, 1, vis), lambda step: (step, 0, 0)),
            pl.BlockSpec((group, patch_count, feats), lambda step: (step, 0, 0)),
        ],
        out_specs=[pl.BlockSpec((group * vis, feats), lambda step: (step, 0))]
        + [whole(shape) for shape in shapes],
        out_shape=[struct((images * vis, feats))] + [struct(shape) for shape in shapes],
        compiler_params=PARAMS,
        cost_estimate=cost(2 * TOK * patch_count * feats, 12 << 20),
        name="prepare",
    )(block_perm[None, :], visible[:, None, :], patches)


def up_kernel(tokens_ref, pieces_ref, place_ref, rep_ref, mask_ref, matrix_ref, section_ref):
    @pl.when(pl.program_id(0) == 0)
    def _():
        pieces = pieces_ref[...].reshape(ALL_ROWS, 128)
        flat = mm(pieces, place_ref[...], 0, 0).astype(BF16)
        matrix_ref[...] = mm(rep_ref[...], flat).astype(BF16) * mask_ref[...]

    section_ref[...] = mm(matrix_ref[...], tokens_ref[...], 1, 1).astype(BF16)


def down_kernel(upstream_ref, pieces_ref, place_ref, spread_ref, mask_ref, matrix_ref, section_ref):
    @pl.when(pl.program_id(0) == 0)
    def _():
        pieces = pieces_ref[...].reshape(ALL_ROWS, 128)
        tall = mm(place_ref[...], pieces, 0, 0).astype(BF16)
        matrix_ref[...] = mm(tall, spread_ref[...]).astype(BF16) * mask_ref[...]

    section_ref[...] = mm(matrix_ref[...], upstream_ref[...], 1, 1).astype(BF16)


def block_map(kernel, name, rows, pieces, place, spread, mask):
    return pl.pallas_call(
        kernel,
        grid=(WIDE_STEPS,),
        in_specs=[
            token_rows(),
            piece_rows(0),
            whole(place.shape),
            whole(spread.shape),
            whole(mask.shape),
        ],
        out_specs=[whole((FEAT, FEAT)), columns(FEAT, WIDE)],
        out_shape=[struct((FEAT, FEAT)), struct((FEAT, TOK))],
        compiler_params=PARAMS,
        cost_estimate=cost(2 * TOK * FEAT * FEAT * 3, 5 << 20),
        name=name,
    )(rows, pieces, place, spread, mask)


def arrange_kernel(two_ref, one_ref, owner_ref, right_one_ref, right_two_ref):
    for pos in range(POS // 2):
        rows = two_ref[:, pos * 16 : pos * 16 + 16, :].reshape(HB, 128)
        right_two_ref[pos] = rows[:, :NB]
        right_two_ref[pos + POS // 2] = rows[:, NB:]
    both = mm(owner_ref[...], one_ref[...].reshape(ALL_ROWS, 128), 0, 0).astype(BF16)
    for pos in range(POS):
        right_one_ref[pos] = jnp.concatenate(
            [both[pos * NB : pos * NB + NB], both[FEAT + pos * NB : FEAT + pos * NB + NB]], axis=1
        )


def arrange(pieces, owner):
    return pl.pallas_call(
        arrange_kernel,
        grid=(1,),
        in_specs=[piece_rows(1), piece_rows(2), whole((ALL_ROWS, ALL_ROWS))],
        out_specs=[whole((POS, NB, HB)), whole((POS, HB, NB))],
        out_shape=[struct((POS, NB, HB)), struct((POS, HB, NB))],
        compiler_params=PARAMS,
        cost_estimate=cost(2 * ALL_ROWS * ALL_ROWS * 128, 3 << 20),
        name="arrange",
    )(pieces, pieces, owner)


def forward_kernel(
    arrived_ref, perm_ref, right_one_ref, right_two_ref, mixed_ref, act_ref, slope_ref, leaving_ref, own_ref
):
    mixed_ref[...] = mm(perm_ref[...], arrived_ref[...], 0, 0).astype(BF16)
    for pos in range(POS):
        rows = slice(pos * NB, (pos + 1) * NB)
        hidden_rows = slice(pos * HB, (pos + 1) * HB)
        hidden = mm(right_one_ref[pos], mixed_ref[rows, :], 0, 0)
        square = hidden * hidden
        tangent = jnp.tanh(hidden * (ROOT_RATIO + (ROOT_RATIO * 0.044715) * square))
        half = 0.5 * hidden
        act = (half + half * tangent).astype(BF16)
        slope = (0.5 + 0.5 * tangent) + half * (1.0 - tangent * tangent) * (
            ROOT_RATIO + (ROOT_RATIO * 3.0 * 0.044715) * square
        )
        act_ref[hidden_rows, :] = act
        slope_ref[hidden_rows, :] = slope.astype(BF16)
        own_ref[rows, :] = mm(right_two_ref[pos], act, 0, 0).astype(BF16)
    leaving_ref[...] = mm(perm_ref[...], own_ref[...]).astype(BF16)


def mix_forward(arrived, perm, right_one, right_two):
    return pl.pallas_call(
        forward_kernel,
        grid=(STEPS,),
        in_specs=[
            columns(FEAT),
            whole((FEAT, FEAT)),
            whole((POS, NB, HB)),
            whole((POS, HB, NB)),
        ],
        out_specs=[columns(FEAT), columns(POS * HB), columns(POS * HB), columns(FEAT)],
        out_shape=[
            struct((FEAT, TOK)),
            struct((POS * HB, TOK)),
            struct((POS * HB, TOK)),
            struct((FEAT, TOK)),
        ],
        scratch_shapes=[pltpu.VMEM((FEAT, TILE), BF16)],
        compiler_params=PARAMS,
        cost_estimate=cost(12 * TOK * FEAT * FEAT, 17 << 20),
        name="mix_forward",
    )(arrived, perm, right_one, right_two)


def backward_kernel(
    me_ref,
    arrived_ref,
    perm_ref,
    right_one_ref,
    right_two_ref,
    mixed_ref,
    act_ref,
    slope_ref,
    owner_ref,
    leaving_ref,
    shares_ref,
    grads_ref,
    own_ref,
    sum_one_ref,
    sum_two_ref,
    pair_ref,
    one_ref,
):
    step = pl.program_id(0)

    @pl.when(step == 0)
    def _():
        sum_one_ref[...] = jnp.zeros_like(sum_one_ref)
        sum_two_ref[...] = jnp.zeros_like(sum_two_ref)

    grads_ref[...] = mm(perm_ref[...], arrived_ref[...], 0, 0).astype(BF16)
    for pos in range(POS):
        rows = slice(pos * NB, (pos + 1) * NB)
        hidden_rows = slice(pos * HB, (pos + 1) * HB)
        grad_act = mm(right_two_ref[pos], grads_ref[rows, :])
        grad_hidden = (grad_act * slope_ref[hidden_rows, :].astype(F32)).astype(BF16)
        own_ref[rows, :] = mm(right_one_ref[pos], grad_hidden).astype(BF16)
        sum_one_ref[rows, :] += mm(mixed_ref[rows, :], grad_hidden, 1, 1)
        sum_two_ref[pos] += mm(act_ref[hidden_rows, :], grads_ref[rows, :], 1, 1)
    leaving_ref[...] = mm(perm_ref[...], own_ref[...]).astype(BF16)

    @pl.when(step == STEPS - 1)
    def _():
        me = me_ref[0]
        halves = jnp.concatenate([sum_one_ref[:, :128], sum_one_ref[:, 128:]], axis=0)
        one_ref[...] = mm(owner_ref[...], halves.astype(BF16)).astype(BF16)
        for pos in range(POS // 2):
            pair_ref[pos] = jnp.concatenate(
                [sum_two_ref[pos], sum_two_ref[pos + POS // 2]], axis=1
            )
        for piece in range(PIECES):
            of = me ^ offset(piece)
            start = pl.multiple_of(of * 16, 16)
            for pos in range(POS // 2):
                shares_ref[piece * 96 + pos * 16 : piece * 96 + pos * 16 + 16, :] = pair_ref[
                    pos, pl.ds(start, 16), :
                ].astype(BF16)
            start = pl.multiple_of(of * 48, 16)
            shares_ref[piece * 96 + 48 : piece * 96 + 96, :] = one_ref[pl.ds(start, 48), :]


def mix_backward(me, arrived, perm, right_one, right_two, mixed, act, slope, owner):
    return pl.pallas_call(
        backward_kernel,
        grid=(STEPS,),
        in_specs=[
            pl.BlockSpec(memory_space=pltpu.SMEM),
            columns(FEAT),
            whole((FEAT, FEAT)),
            whole((POS, NB, HB)),
            whole((POS, HB, NB)),
            columns(FEAT),
            columns(POS * HB),
            columns(POS * HB),
            whole((ALL_ROWS, ALL_ROWS)),
        ],
        out_specs=[columns(FEAT), whole((PIECES * 96, 128))],
        out_shape=[struct((FEAT, TOK)), struct((PIECES * 96, 128))],
        scratch_shapes=[
            pltpu.VMEM((FEAT, TILE), BF16),
            pltpu.VMEM((FEAT, TILE), BF16),
            pltpu.VMEM((FEAT, HB), F32),
            pltpu.VMEM((POS, HB, NB), F32),
            pltpu.VMEM((POS // 2, HB, 2 * NB), F32),
            pltpu.VMEM((ALL_ROWS, 128), BF16),
        ],
        compiler_params=PARAMS,
        cost_estimate=cost(20 * TOK * FEAT * FEAT, 17 << 20),
        name="mix_backward",
    )(me, arrived, perm, right_one, right_two, mixed, act, slope, owner)


def output_kernel(returned_ref, matrix_ref, upstream_ref, mask_ref, fold_ref, out_ref, grad_ref, sum_ref):
    step = pl.program_id(0)

    @pl.when(step == 0)
    def _():
        sum_ref[...] = jnp.zeros_like(sum_ref)

    out_ref[...] = mm(returned_ref[...], matrix_ref[...], 0, 0).astype(BF16)
    sum_ref[...] += mm(returned_ref[...], upstream_ref[...])

    @pl.when(step == WIDE_STEPS - 1)
    def _():
        kept = sum_ref[...].astype(BF16) * mask_ref[...]
        grad_ref[...] = mm(kept, fold_ref[...]).astype(BF16)


def output_and_grad(returned, matrix, upstream, mask, fold):
    return pl.pallas_call(
        output_kernel,
        grid=(WIDE_STEPS,),
        in_specs=[
            columns(FEAT, WIDE),
            whole((FEAT, FEAT)),
            token_rows(),
            whole((FEAT, FEAT)),
            whole((FEAT, 128)),
        ],
        out_specs=[token_rows(), whole((FEAT, 128))],
        out_shape=[struct((TOK, FEAT)), struct((FEAT, 128))],
        scratch_shapes=[pltpu.VMEM((FEAT, FEAT), F32)],
        compiler_params=PARAMS,
        cost_estimate=cost(4 * TOK * FEAT * FEAT, 5 << 20),
        name="output_and_grad",
    )(returned, matrix, upstream, mask, fold)


def first_grad_kernel(
    returned_ref,
    tokens_ref,
    mask_ref,
    rep_ref,
    order_one_ref,
    order_two_ref,
    second_ref,
    shares_ref,
    sum_ref,
):
    step = pl.program_id(0)

    @pl.when(step == 0)
    def _():
        sum_ref[...] = jnp.zeros_like(sum_ref)

    sum_ref[...] += mm(returned_ref[...], tokens_ref[...])

    @pl.when(step == WIDE_STEPS - 1)
    def _():
        kept = sum_ref[...].astype(BF16) * mask_ref[...]
        flat = mm(rep_ref[...], kept, 0, 0).astype(BF16)
        shares = mm(order_one_ref[...], flat, 1, 1) + mm(order_two_ref[...], second_ref[...])
        shares_ref[...] = shares.astype(BF16)


def first_grad(returned, tokens, mask, rep, order_one, order_two, second):
    return pl.pallas_call(
        first_grad_kernel,
        grid=(WIDE_STEPS,),
        in_specs=[
            columns(FEAT, WIDE),
            token_rows(),
            whole((FEAT, FEAT)),
            whole((FEAT, 128)),
            whole((ALL_ROWS, FEAT)),
            whole((ALL_ROWS, FEAT)),
            whole((FEAT, 128)),
        ],
        out_specs=whole((ALL_ROWS, 128)),
        out_shape=struct((ALL_ROWS, 128)),
        scratch_shapes=[pltpu.VMEM((FEAT, FEAT), F32)],
        compiler_params=PARAMS,
        cost_estimate=cost(2 * TOK * FEAT * FEAT, 3 << 20),
        name="first_grad",
    )(returned, tokens, mask, rep, order_one, order_two, second)


def token_grad_kernel(returned_ref, matrix_ref, out_ref):
    out_ref[...] = mm(returned_ref[...], matrix_ref[...], 0, 0).astype(BF16)


def token_gradient(returned, matrix):
    return pl.pallas_call(
        token_grad_kernel,
        grid=(WIDE_STEPS,),
        in_specs=[columns(FEAT, WIDE), whole((FEAT, FEAT))],
        out_specs=token_rows(),
        out_shape=struct((TOK, FEAT)),
        compiler_params=PARAMS,
        cost_estimate=cost(2 * TOK * FEAT * FEAT, 3 << 20),
        name="token_gradient",
    )(returned, matrix)


def exchange(x, bit):
    return lax.ppermute(x, "dp", [(i, i ^ bit) for i in range(PIECES)])


def halved(x, bit):
    rows = x.shape[0] // 2
    return (x[:rows].astype(F32) + exchange(x[rows:], bit).astype(F32)).astype(BF16)


def to_tensor(x):
    return lax.all_to_all(x, "tensor", split_axis=0, concat_axis=0, tiled=True)


def local(
    patches, visible, block_perm, first_left, first_right, second_right, second_left, cotangent
):
    tie = lax.optimization_barrier
    me = lax.axis_index("dp").astype(jnp.int32).reshape(1)

    left = jnp.concatenate([first_left.transpose(1, 0, 2), second_left.transpose(1, 0, 2)], axis=0)
    left = jnp.pad(left.reshape(48, BS), ((0, 0), (0, 128 - BS)))
    two = second_right.reshape(2, 3, 16, NB).transpose(1, 2, 0, 3).reshape(48, 128)
    one = first_right.reshape(24, HB)
    piece = jnp.concatenate([left, two, one[:, :128], one[:, 128:]], axis=0)
    pieces = jnp.broadcast_to(piece[None], (PIECES, 144, 128))
    pieces = lax.all_to_all(pieces, "dp", split_axis=0, concat_axis=0, tiled=True)

    tokens, place_one, place_two, owner, perm, mask, rep, fold, spread = prepare(
        block_perm, visible, patches
    )
    pieces, tokens = tie((pieces, tokens))

    matrix_one, section_one = block_map(
        up_kernel, "first_map", tokens, pieces, place_one, rep, mask
    )
    arrived = to_tensor(section_one)
    matrix_two, back_grad = block_map(
        down_kernel, "second_map_back", cotangent, pieces, place_two, spread, mask
    )
    right_one, right_two = arrange(pieces, owner)
    arrived, back_grad, right_one = tie((arrived, back_grad, right_one))
    arrived_grad = to_tensor(back_grad)

    mixed, act, slope, leaving = mix_forward(arrived, perm, right_one, right_two)
    leaving, arrived_grad = tie((leaving, arrived_grad))
    returned = to_tensor(leaving)
    leaving_grad, right_shares = mix_backward(
        me, arrived_grad, perm, right_one, right_two, mixed, act, slope, owner
    )
    right_shares = halved(right_shares, DP_ORDER[3])
    returned, leaving_grad, right_shares = tie((returned, leaving_grad, right_shares))
    returned_grad = to_tensor(leaving_grad)
    output, grad_left_two = output_and_grad(returned, matrix_two, cotangent, mask, fold)
    right_shares, grad_left_two = tie((right_shares, grad_left_two))
    right_shares = halved(right_shares, DP_ORDER[2])
    right_shares = halved(right_shares, DP_ORDER[1])

    left_held = first_grad(
        returned_grad, tokens, mask, rep, place_one, place_two, grad_left_two
    )
    left_shares = lax.all_to_all(left_held, "dp", split_axis=0, concat_axis=0, tiled=True)
    returned_grad, left_held = tie((returned_grad, left_held))
    token_grad = token_gradient(returned_grad, matrix_one)

    right_total = halved(right_shares, DP_ORDER[0]).astype(F32)

    left_total = jnp.sum(left_shares.reshape(PIECES, 48, 128).astype(F32), axis=0)[:, :BS]
    left_total = left_total.reshape(2, 6, LB, BS).transpose(0, 2, 1, 3)
    two_total = right_total[:48].reshape(3, 16, 2, NB).transpose(2, 0, 1, 3).reshape(POS, 16, NB)
    one_total = jnp.concatenate([right_total[48:72], right_total[72:]], axis=1)
    one_total = one_total.reshape(POS, 4, HB)
    return (output, token_grad, left_total[0], one_total, two_total, left_total[1])


def solution(mesh):
    placed = (
        P("dp", None, "tensor"),
        P("dp", None),
        P(),
        P("tensor", "dp", None),
        P("tensor", "dp", None),
        P("tensor", "dp", None),
        P("tensor", "dp", None),
        P("dp", "tensor"),
    )
    return jax.shard_map(
        local,
        mesh=mesh,
        in_specs=placed,
        out_specs=(
            P("dp", "tensor"),
            P("dp", "tensor"),
            P("tensor", "dp", None),
            P("tensor", "dp", None),
            P("tensor", "dp", None),
            P("tensor", "dp", None),
        ),
        check_vma=False,
    )
```

time: 252 us -> 178 us (0.71)
  local copies, waits for them, and re-layouts: 60.3 us -> 6.21 us
  blocking collectives: 26.3 us -> 0 us
  Pallas kernels: 46.5 us -> 65.6 us
  other arithmetic: 18 us -> 1.81 us
  waiting for transfers between devices: 54.2 us -> 61.3 us
  starting transfers between devices: 43.4 us -> 40.5 us
    unnamed x142 -> x2, local copies, waits for them, and re-layouts: 41.6 us -> 0.85 us
    all_to_all x1 -> x0, blocking collectives: 26.3 us -> none  [to_tensor(): return lax.all_to_all(x, 'tensor', split_axis=0, concat_axis=0, tiled=True)]
    pallas_call x7 -> x8, Pallas kernels: 30 us -> 48.1 us  [the longest x1 15.7 us: mix_backward(): pl.pallas_call(backward_kernel, grid=(STEPS,), in_specs=[pl.BlockSpec(mem...]
    ppermute x8 -> x4, starting transfers between devices: 18.1 us -> 3.49 us  [exchange(): return lax.ppermute(x, 'dp', [(i, i ^ bit) for i in range(PIECES)])]
    convert_element_type x7 -> x4, other arithmetic: 10.7 us -> 1.04 us  [the longest x3 1.03 us: halved(): (x[:rows].astype(F32) + exchange(x[rows:], bit).astype(F32)).astype(BF16)]
    all_to_all x1 -> x2, starting transfers between devices: 8.33 us -> 14.2 us  [the longest x1 10.1 us: local(): lax.all_to_all(pieces, 'dp', split_axis=0, concat_axis=0, tiled=True)]
    all_to_all x3 -> x4, starting transfers between devices: 17.1 us -> 22.8 us  [to_tensor(): return lax.all_to_all(x, 'tensor', split_axis=0, concat_axis=0, tiled=True)]
    reshape x8 -> x2, local copies, waits for them, and re-layouts: 5 us -> 0.71 us  [the longest x1 0.62 us: local(): one_total = one_total.reshape(POS, 4, HB)]
  transfers between devices with their start and end apart: 12 -> 10, of which waited for: 6 -> 8; matrix products, arithmetic and copies ran while one was open for 16% -> 2% of each run, Pallas kernels for 11% -> 32%
where the time goes in v2:
time: 178 us; the launch traced here: 176 us
  Pallas kernels  65.6 us (37%)
  waiting for transfers between devices  61.3 us (34%)
  starting transfers between devices  40.5 us (23%)
  local copies, waits for them, and re-layouts  6.21 us (3%)
  other arithmetic  1.81 us (1%)
    ppermute x4, waiting for transfers between devices, exchange(): return lax.ppermute(x, 'dp', [(i, i ^ bit) for i in range(PIECES)])  24.9 us
    all_to_all x4, starting transfers between devices, to_tensor(): return lax.all_to_all(x, 'tensor', split_axis=0, concat_axis=0, tiled=True)  22.8 us
    all_to_all x4, waiting for transfers between devices, to_tensor(): return lax.all_to_all(x, 'tensor', split_axis=0, concat_axis=0, tiled=True)  17.6 us
    pallas_call x1, Pallas kernels, mix_forward(): pl.pallas_call(forward_kernel, grid=(STEPS,), in_specs=[columns(FEAT), wh...  17.5 us
    pallas_call x1, Pallas kernels, mix_backward(): pl.pallas_call(backward_kernel, grid=(STEPS,), in_specs=[pl.BlockSpec(mem...  15.7 us
    all_to_all x1, waiting for transfers between devices, local(): lax.all_to_all(pieces, 'dp', split_axis=0, concat_axis=0, tiled=True)  12 us
    all_to_all x1, starting transfers between devices, local(): lax.all_to_all(pieces, 'dp', split_axis=0, concat_axis=0, tiled=True)  10.1 us
    pallas_call x2, Pallas kernels, block_map(): pl.pallas_call(kernel, grid=(WIDE_STEPS,), in_specs=[token_rows(), piece_...  8.47 us
  transfers between devices with their start and end apart: 10, of which 8 were waited for; matrix products, arithmetic and copies ran while one was open for 2% of the time, Pallas kernels for 32%

profile of v2, /device:TPU:2, one launch (start us, length us, event | category | flops | bytes accessed | tf_op | source)
XLA Modules:
  0.0 176.2 jit_solution(11177992640505539340)
XLA Ops:
  0.6 0.7 reshape.55
  1.4 0.8 copy.14
  2.1 0.1 reshape.54
  2.2 0.7 pad_maximum_fusion.1
  2.9 0.9 broadcast_in_dim.12
  3.8 10.1 %all-to-all-start = ((bf16[16,144,128]{2,1,0:T(8,128)(2,1)}), bf16[16,144,128]{2,1,0:T(8,128)(2,1)S(1)}, u32[]{:S(2)}, u32[]{:S(2)}) async-start(bf16[16,144,128]{2,1,0:T(8,128)(2,1)} %broadcast_in_dim.12), calls=%async_computation | async-start | bytes 1179648 | tf_op jit(solution)/shard_map/all_to_all | solution.py:485
  14.0 8.3 %prepare.1 = (bf16[2048,384]{1,0:T(8,128)(2,1)}, bf16[768,384]{1,0:T(8,128)(2,1)}, bf16[768,384]{1,0:T(8,128)(2,1)}, bf16[768,768]{1,0:T(8,128)(2,1)}, bf16[384,...) custom-call(s32[1,64]{1,0:T(1,128)} %bitcast.41, ...), custom_call_target="tpu_custom_call" | custom-call | flops 402653184 | bytes 12582912 | tf_op jit(solution)/shard_map/prepare/pallas_call | solution.py:144
  22.2 12.0 %all-to-all-done.pieces_ref.two_ref.one_ref = bf16[16,144,128]{2,1,0:T(8,128)(2,1)S(1)} async-done(((bf16[16,144,128]{2,1,0:T(8,128)(2,1)}), bf16[16,144,128]{2,1,0:T(8,128)(2,1)S(1)}, u32[]{:S(2)}, u32[]{:S(2)}) %all-to-all-start) | async-done | bytes 589856 | tf_op jit(solution)/shard_map/all_to_all | solution.py:485
  34.3 0.0 copy-start
  34.3 0.8 copy-done
  35.1 4.1 %first_map.1 = (bf16[384,384]{1,0:T(8,128)(2,1)}, bf16[384,2048]{1,0:T(8,128)(2,1)}) custom-call(bf16[2048,384]{1,0:T(8,128)(2,1)} %get-tuple-element.43.tokens_ref, bf16[16,144,128]{2,1,0:T(8,128)(2,1)} %copy-done, bf16[768,384]{1,0:T(8,128)(2,1)} %get-tuple-element.45.place_ref.order_one_ref, bf16[384,128]{1,0:T(8,128)(2,1)} %get-tuple-element.46.rep_ref, ...), custom_call_target="tpu_custom_call" | custom-call | flops 1811939328 | bytes 5242880 | tf_op jit(solution)/shard_map/first_map/pallas_call | solution.py:182
  39.2 6.0 %all-to-all-start.1 = ((bf16[16,24,2048]{2,1,0:T(8,128)(2,1)}), bf16[16,24,2048]{2,1,0:T(8,128)(2,1)}, u32[]{:S(2)}, u32[]{:S(2)}) async-start(bf16[16,24,2048]{2,1,0:T(8,128)(2,1)} %bitcast.31), calls=%async_computation.1 | async-start | bytes 3145728 | tf_op jit(solution)/shard_map/all_to_all | solution.py:470
  45.2 2.9 %arrange.1 = (bf16[6,64,256]{2,1,0:T(8,128)(2,1)}, bf16[6,256,64]{2,1,0:T(8,128)(2,1)}) custom-call(bf16[16,144,128]{2,1,0:T(8,128)(2,1)} %copy-done, bf16[16,144,128]{2,1,0:T(8,128)(2,1)} %copy-done, bf16[768,768]{1,0:T(8,128)(2,1)} %get-tuple-element.52.owner_ref), custom_call_target="tpu_custom_call" | custom-call | flops 150994944 | bytes 3145728 | tf_op jit(solution)/shard_map/arrange/pallas_call | solution.py:213
  48.0 4.3 %second_map_back.1 = (bf16[384,384]{1,0:T(8,128)(2,1)}, bf16[384,2048]{1,0:T(8,128)(2,1)}) custom-call(bf16[2048,384]{1,0:T(8,128)(2,1)} %upstream_ref.3, bf16[16,144,128]{2,1,0:T(8,128)(2,1)} %copy-done, bf16[768,384]{1,0:T(8,128)(2,1)} %get-tuple-element.49.place_ref.order_two_ref, bf16[128,384]{1,0:T(8,128)(2,1)} %get-tuple-element.50.spread_ref, ...), custom_call_target="tpu_custom_call" | custom-call | flops 1811939328 | bytes 5242880 | tf_op jit(solution)/shard_map/second_map_back/pallas_call | solution.py:182
  52.4 13.9 %all-to-all-done.1 = bf16[16,24,2048]{2,1,0:T(8,128)(2,1)} async-done(((bf16[16,24,2048]{2,1,0:T(8,128)(2,1)}), bf16[16,24,2048]{2,1,0:T(8,128)(2,1)}, u32[]{:S(2)}, u32[]{:S(2)}) %all-to-all-start.1) | async-done | bytes 1572896 | tf_op jit(solution)/shard_map/all_to_all | solution.py:470
  66.3 5.5 %all-to-all-start.2 = ((bf16[16,24,2048]{2,1,0:T(8,128)(2,1)}), bf16[16,24,2048]{2,1,0:T(8,128)(2,1)}, u32[]{:S(2)}, u32[]{:S(2)}) async-start(bf16[16,24,2048]{2,1,0:T(8,128)(2,1)} %bitcast.30), calls=%async_computation.2 | async-start | bytes 3145728 | tf_op jit(solution)/shard_map/all_to_all | solution.py:470
  71.8 17.5 %mix_forward.1 = (bf16[384,2048]{1,0:T(8,128)(2,1)}, bf16[1536,2048]{1,0:T(8,128)(2,1)}, bf16[1536,2048]{1,0:T(8,128)(2,1)}, bf16[384,2048]{1,0:T(8,128)(2,1)}) custom-call(bf16[384,2048]{1,0:T(8,128)(2,1)} %bitcast.8.arrived_ref, bf16[384,384]{1,0:T(8,128)(2,1)} %get-tuple-element.55.perm_ref, bf16[6,64,256]{2,1,0:T(8,128)(2,1)} %get-tuple-element.56.right_one_ref, ...), custom_call_target="tpu_custom_call" | custom-call | flops 3623878656 | bytes 17825792 | tf_op jit(solution)/shard_map/mix_forward/pallas_call | solution.py:247
  89.3 3.7 %all-to-all-done.2 = bf16[16,24,2048]{2,1,0:T(8,128)(2,1)} async-done(((bf16[16,24,2048]{2,1,0:T(8,128)(2,1)}), bf16[16,24,2048]{2,1,0:T(8,128)(2,1)}, u32[]{:S(2)}, u32[]{:S(2)}) %all-to-all-start.2) | async-done | bytes 1572896 | tf_op jit(solution)/shard_map/all_to_all | solution.py:470
  93.0 5.5 %all-to-all-start.3 = ((bf16[16,24,2048]{2,1,0:T(8,128)(2,1)}), bf16[16,24,2048]{2,1,0:T(8,128)(2,1)}, u32[]{:S(2)}, u32[]{:S(2)}) async-start(bf16[16,24,2048]{2,1,0:T(8,128)(2,1)} %bitcast.29), calls=%async_computation.3 | async-start | bytes 3145728 | tf_op jit(solution)/shard_map/all_to_all | solution.py:470
  98.5 15.7 %mix_backward.1 = (bf16[384,2048]{1,0:T(8,128)(2,1)}, bf16[1536,128]{1,0:T(8,128)(2,1)}) custom-call(s32[1]{0:T(128)} %bitcast.13.me_ref, bf16[384,2048]{1,0:T(8,128)(2,1)} %bitcast.10.arrived_ref, bf16[384,384]{1,0:T(8,128)(2,1)} %get-tuple-element.55.perm_ref, bf16[6,64,256]{2,1,0:T(8,128)(2,1)} %get-tuple-element.56.right_one_ref, ...), custom_call_target="tpu_custom_call" | custom-call | flops 6039797760 | bytes 17825792 | tf_op jit(solution)/shard_map/mix_backward/pallas_call | solution.py:328
  114.2 0.9 slice.51
  115.2 0.3 collective-permute-start
  115.4 6.9 %collective-permute-done = bf16[768,128]{1,0:T(8,128)(2,1)S(1)} collective-permute-done((bf16[768,128]{1,0:T(8,128)(2,1)S(1)}, bf16[768,128]{1,0:T(8,128)(2,1)S(1)}, u32[]{:S(2)}, u32[]{:S(2)}) %collective-permute-start) | collective-permute-done | bytes 196640 | tf_op jit(solution)/shard_map/ppermute | solution.py:461
  122.4 1.0 add_convert_fusion
  123.4 0.0 all-to-all-done.3
  123.4 5.8 %all-to-all-start.4 = ((bf16[16,24,2048]{2,1,0:T(8,128)(2,1)}), bf16[16,24,2048]{2,1,0:T(8,128)(2,1)}, u32[]{:S(2)}, u32[]{:S(2)}) async-start(bf16[16,24,2048]{2,1,0:T(8,128)(2,1)} %bitcast.28), calls=%async_computation.4 | async-start | bytes 3145728 | tf_op jit(solution)/shard_map/all_to_all | solution.py:470
  129.2 5.0 %output_and_grad.1 = (bf16[2048,384]{1,0:T(8,128)(2,1)}, bf16[384,128]{1,0:T(8,128)(2,1)}) custom-call(bf16[384,2048]{1,0:T(8,128)(2,1)} %bitcast.12.returned_ref, bf16[384,384]{1,0:T(8,128)(2,1)} %get-tuple-element.68.matrix_ref, bf16[2048,384]{1,0:T(8,128)(2,1)} %upstream_ref.3, bf16[384,384]{1,0:T(8,128)(2,1)} %get-tuple-element.47.mask_ref, ...), custom_call_target="tpu_custom_call" | custom-call | flops 1207959552 | bytes 5242880 | tf_op jit(solution)/shard_map/output_and_grad/pallas_call | solution.py:375
  134.1 0.8 collective-permute-start.1
  134.9 6.9 %collective-permute-done.1 = bf16[384,128]{1,0:T(8,128)(2,1)S(1)} collective-permute-done((bf16[384,128]{1,0:T(8,128)(2,1)S(1)}, bf16[384,128]{1,0:T(8,128)(2,1)S(1)}, u32[]{:S(2)}, u32[]{:S(2)}) %collective-permute-start.1) | collective-permute-done | bytes 98336 | tf_op jit(solution)/shard_map/ppermute | solution.py:461
  141.9 1.9 %collective-permute-start.2 = (bf16[192,128]{1,0:T(8,128)(2,1)S(1)}, bf16[192,128]{1,0:T(8,128)(2,1)S(1)}, u32[]{:S(2)}, u32[]{:S(2)}) collective-permute-start(bf16[192,128]{1,0:T(8,128)(2,1)S(1)} %slice.69), channel_id=1, source_target_pairs={{0,128},{16,144},{32,160},{48,176},{64,192},{80,208},{96,224},{112... | collective-permute-start | bytes 147464 | tf_op jit(solution)/shard_map/ppermute | solution.py:461
  143.7 6.2 %collective-permute-done.2 = bf16[192,128]{1,0:T(8,128)(2,1)S(1)} collective-permute-done((bf16[192,128]{1,0:T(8,128)(2,1)S(1)}, bf16[192,128]{1,0:T(8,128)(2,1)S(1)}, u32[]{:S(2)}, u32[]{:S(2)}) %collective-permute-start.2) | collective-permute-done | bytes 49184 | tf_op jit(solution)/shard_map/ppermute | solution.py:461
  150.0 0.6 collective-permute-start.3
  150.5 4.9 %collective-permute-done.3 = bf16[96,128]{1,0:T(8,128)(2,1)S(1)} collective-permute-done((bf16[96,128]{1,0:T(8,128)(2,1)S(1)}, bf16[96,128]{1,0:T(8,128)(2,1)S(1)}, u32[]{:S(2)}, u32[]{:S(2)}) %collective-permute-start.3) | collective-permute-done | bytes 24608 | tf_op jit(solution)/shard_map/ppermute | solution.py:461
  155.4 0.0 all-to-all-done.4
  155.4 4.4 %first_grad.1 = bf16[768,128]{1,0:T(8,128)(2,1)} custom-call(bf16[384,2048]{1,0:T(8,128)(2,1)} %bitcast.15.returned_ref, bf16[2048,384]{1,0:T(8,128)(2,1)} %get-tuple-element.43.tokens_ref, bf16[384,384]{1,0:T(8,128)(2,1)} %get-tuple-element.47.mask_ref, bf16[384,128]{1,0:T(8,128)(2,1)} %get-tuple-element.46.rep_ref, ...), custom_call_target="tpu_custom_call" | custom-call | flops 603979776 | bytes 3145728 | tf_op jit(solution)/shard_map/first_grad/pallas_call | solution.py:422
  159.8 4.1 %all-to-all-start.5 = ((bf16[16,48,128]{2,1,0:T(8,128)(2,1)}), bf16[16,48,128]{2,1,0:T(8,128)(2,1)S(1)}, u32[]{:S(2)}, u32[]{:S(2)}) async-start(bf16[16,48,128]{2,1,0:T(8,128)(2,1)} %bitcast.32), calls=%async_computation.5 | async-start | bytes 393216 | tf_op jit(solution)/shard_map/all_to_all | solution.py:520
  163.9 0.6 reshape.58
  164.5 0.1 reshape.59
  164.6 0.6 copy.15
  165.2 3.5 %token_gradient.1 = bf16[2048,384]{1,0:T(8,128)(2,1)} custom-call(bf16[384,2048]{1,0:T(8,128)(2,1)} %bitcast.15.returned_ref, bf16[384,384]{1,0:T(8,128)(2,1)} %get-tuple-element.76.matrix_ref), custom_call_target="tpu_custom_call" | custom-call | flops 603979776 | bytes 3145728 | tf_op jit(solution)/shard_map/token_gradient/pallas_call | solution.py:448
  168.7 6.8 %all-to-all-done.5 = bf16[16,48,128]{2,1,0:T(8,128)(2,1)S(1)} async-done(((bf16[16,48,128]{2,1,0:T(8,128)(2,1)}), bf16[16,48,128]{2,1,0:T(8,128)(2,1)S(1)}, u32[]{:S(2)}, u32[]{:S(2)}) %all-to-all-start.5) | async-done | bytes 196640 | tf_op jit(solution)/shard_map/all_to_all | solution.py:520
  175.6 0.6 slice_bitcast_fusion
  (12 shorter events, 0.1 us)
Async XLA Ops:
  3.8 30.4 %all-to-all-start = ((bf16[16,144,128]{2,1,0:T(8,128)(2,1)}), bf16[16,144,128]{2,1,0:T(8,128)(2,1)S(1)}, u32[]{:S(2)}, u32[]{:S(2)}) async-start(bf16[16,144,128]{2,1,0:T(8,128)(2,1)} %broadcast_in_dim.12), calls=%async_computation | async-start | bytes 1179648 | tf_op jit(solution)/shard_map/all_to_all | solution.py:485
  34.3 0.8 copy-start
  39.2 27.1 %all-to-all-start.1 = ((bf16[16,24,2048]{2,1,0:T(8,128)(2,1)}), bf16[16,24,2048]{2,1,0:T(8,128)(2,1)}, u32[]{:S(2)}, u32[]{:S(2)}) async-start(bf16[16,24,2048]{2,1,0:T(8,128)(2,1)} %bitcast.31), calls=%async_computation.1 | async-start | bytes 3145728 | tf_op jit(solution)/shard_map/all_to_all | solution.py:470
  66.3 26.7 %all-to-all-start.2 = ((bf16[16,24,2048]{2,1,0:T(8,128)(2,1)}), bf16[16,24,2048]{2,1,0:T(8,128)(2,1)}, u32[]{:S(2)}, u32[]{:S(2)}) async-start(bf16[16,24,2048]{2,1,0:T(8,128)(2,1)} %bitcast.30), calls=%async_computation.2 | async-start | bytes 3145728 | tf_op jit(solution)/shard_map/all_to_all | solution.py:470
  93.0 30.4 %all-to-all-start.3 = ((bf16[16,24,2048]{2,1,0:T(8,128)(2,1)}), bf16[16,24,2048]{2,1,0:T(8,128)(2,1)}, u32[]{:S(2)}, u32[]{:S(2)}) async-start(bf16[16,24,2048]{2,1,0:T(8,128)(2,1)} %bitcast.29), calls=%async_computation.3 | async-start | bytes 3145728 | tf_op jit(solution)/shard_map/all_to_all | solution.py:470
  115.2 7.2 %collective-permute-start = (bf16[768,128]{1,0:T(8,128)(2,1)S(1)}, bf16[768,128]{1,0:T(8,128)(2,1)S(1)}, u32[]{:S(2)}, u32[]{:S(2)}) collective-permute-start(bf16[768,128]{1,0:T(8,128)(2,1)S(1)} %slice.51), channel_id=1, source_target_pairs={{0,32},{16,48},{32,0},{48,16},{64,96},{80,112},{96,64},{112,80},{1... | collective-permute-start | bytes 589832 | tf_op jit(solution)/shard_map/ppermute | solution.py:461
  123.4 32.0 %all-to-all-start.4 = ((bf16[16,24,2048]{2,1,0:T(8,128)(2,1)}), bf16[16,24,2048]{2,1,0:T(8,128)(2,1)}, u32[]{:S(2)}, u32[]{:S(2)}) async-start(bf16[16,24,2048]{2,1,0:T(8,128)(2,1)} %bitcast.28), calls=%async_computation.4 | async-start | bytes 3145728 | tf_op jit(solution)/shard_map/all_to_all | solution.py:470
  134.1 7.7 %collective-permute-start.1 = (bf16[384,128]{1,0:T(8,128)(2,1)S(1)}, bf16[384,128]{1,0:T(8,128)(2,1)S(1)}, u32[]{:S(2)}, u32[]{:S(2)}) collective-permute-start(bf16[384,128]{1,0:T(8,128)(2,1)S(1)} %slice.55), channel_id=1, source_target_pairs={{0,64},{16,80},{32,96},{48,112},{64,0},{80,16},{96,32},{112,48},{1... | collective-permute-start | bytes 294920 | tf_op jit(solution)/shard_map/ppermute | solution.py:461
  141.9 8.1 %collective-permute-start.2 = (bf16[192,128]{1,0:T(8,128)(2,1)S(1)}, bf16[192,128]{1,0:T(8,128)(2,1)S(1)}, u32[]{:S(2)}, u32[]{:S(2)}) collective-permute-start(bf16[192,128]{1,0:T(8,128)(2,1)S(1)} %slice.69), channel_id=1, source_target_pairs={{0,128},{16,144},{32,160},{48,176},{64,192},{80,208},{96,224},{112... | collective-permute-start | bytes 147464 | tf_op jit(solution)/shard_map/ppermute | solution.py:461
  150.0 5.4 %collective-permute-start.3 = (bf16[96,128]{1,0:T(8,128)(2,1)S(1)}, bf16[96,128]{1,0:T(8,128)(2,1)S(1)}, u32[]{:S(2)}, u32[]{:S(2)}) collective-permute-start(bf16[96,128]{1,0:T(8,128)(2,1)S(1)} %slice.71), channel_id=1, source_target_pairs={{0,16},{16,0},{32,48},{48,32},{64,80},{80,64},{96,112},{112,96},{1... | collective-permute-start | bytes 73736 | tf_op jit(solution)/shard_map/ppermute | solution.py:461
  159.8 15.8 %all-to-all-start.5 = ((bf16[16,48,128]{2,1,0:T(8,128)(2,1)}), bf16[16,48,128]{2,1,0:T(8,128)(2,1)S(1)}, u32[]{:S(2)}, u32[]{:S(2)}) async-start(bf16[16,48,128]{2,1,0:T(8,128)(2,1)} %bitcast.32), calls=%async_computation.5 | async-start | bytes 393216 | tf_op jit(solution)/shard_map/all_to_all | solution.py:520

commit v3 on v2

--- a/solution.py
+++ b/solution.py
@@ -16,13 +16,13 @@
 TOK = 2048
 PIECES = 16
 ALL_ROWS = 768
-TILE = 512
+TILE = 1024
 STEPS = TOK // TILE
 WIDE = 1024
 WIDE_STEPS = TOK // WIDE
 ROOT_RATIO = math.sqrt(2.0 / math.pi)
 DP_ORDER = (1, 8, 4, 2)
-PARAMS = pltpu.CompilerParams(vmem_limit_bytes=63 * 1024 * 1024)
+PARAMS = pltpu.CompilerParams(vmem_limit_bytes=63 * 1024 * 1024 + 512 * 1024)
 
 
 def mm(lhs, rhs, left_dim=1, right_dim=0):
@@ -278,7 +278,8 @@
     slope_ref,
     owner_ref,
     leaving_ref,
-    shares_ref,
+    kept_ref,
+    sent_ref,
     grads_ref,
     own_ref,
     sum_one_ref,
@@ -316,12 +317,14 @@
         for piece in range(PIECES):
             of = me ^ offset(piece)
             start = pl.multiple_of(of * 16, 16)
+            shares_ref = (kept_ref, sent_ref)[piece // 8]
+            at = piece % 8 * 96
             for pos in range(POS // 2):
-                shares_ref[piece * 96 + pos * 16 : piece * 96 + pos * 16 + 16, :] = pair_ref[
+                shares_ref[at + pos * 16 : at + pos * 16 + 16, :] = pair_ref[
                     pos, pl.ds(start, 16), :
                 ].astype(BF16)
             start = pl.multiple_of(of * 48, 16)
-            shares_ref[piece * 96 + 48 : piece * 96 + 96, :] = one_ref[pl.ds(start, 48), :]
+            shares_ref[at + 48 : at + 96, :] = one_ref[pl.ds(start, 48), :]
 
 
 def mix_backward(me, arrived, perm, right_one, right_two, mixed, act, slope, owner):
@@ -339,8 +342,8 @@
             columns(POS * HB),
             whole((ALL_ROWS, ALL_ROWS)),
         ],
-        out_specs=[columns(FEAT), whole((PIECES * 96, 128))],
-        out_shape=[struct((FEAT, TOK)), struct((PIECES * 96, 128))],
+        out_specs=[columns(FEAT), whole((ALL_ROWS, 128)), whole((ALL_ROWS, 128))],
+        out_shape=[struct((FEAT, TOK)), struct((ALL_ROWS, 128)), struct((ALL_ROWS, 128))],
         scratch_shapes=[
             pltpu.VMEM((FEAT, TILE), BF16),
             pltpu.VMEM((FEAT, TILE), BF16),
@@ -355,14 +358,13 @@
     )(me, arrived, perm, right_one, right_two, mixed, act, slope, owner)
 
 
-def output_kernel(returned_ref, matrix_ref, upstream_ref, mask_ref, fold_ref, out_ref, grad_ref, sum_ref):
+def second_grad_kernel(returned_ref, upstream_ref, mask_ref, fold_ref, grad_ref, sum_ref):
     step = pl.program_id(0)
 
     @pl.when(step == 0)
     def _():
         sum_ref[...] = jnp.zeros_like(sum_ref)
 
-    out_ref[...] = mm(returned_ref[...], matrix_ref[...], 0, 0).astype(BF16)
     sum_ref[...] += mm(returned_ref[...], upstream_ref[...])
 
     @pl.when(step == WIDE_STEPS - 1)
@@ -371,24 +373,18 @@
         grad_ref[...] = mm(kept, fold_ref[...]).astype(BF16)
 
 
-def output_and_grad(returned, matrix, upstream, mask, fold):
-    return pl.pallas_call(
-        output_kernel,
+def second_grad(returned, upstream, mask, fold):
+    return pl.pallas_call(
+        second_grad_kernel,
         grid=(WIDE_STEPS,),
-        in_specs=[
-            columns(FEAT, WIDE),
-            whole((FEAT, FEAT)),
-            token_rows(),
-            whole((FEAT, FEAT)),
-            whole((FEAT, 128)),
-        ],
-        out_specs=[token_rows(), whole((FEAT, 128))],
-        out_shape=[struct((TOK, FEAT)), struct((FEAT, 128))],
+        in_specs=[columns(FEAT, WIDE), token_rows(), whole((FEAT, FEAT)), whole((FEAT, 128))],
+        out_specs=whole((FEAT, 128)),
+        out_shape=struct((FEAT, 128)),
         scratch_shapes=[pltpu.VMEM((FEAT, FEAT), F32)],
         compiler_params=PARAMS,
-        cost_estimate=cost(4 * TOK * FEAT * FEAT, 5 << 20),
-        name="output_and_grad",
-    )(returned, matrix, upstream, mask, fold)
+        cost_estimate=cost(2 * TOK * FEAT * FEAT, 4 << 20),
+        name="second_grad",
+    )(returned, upstream, mask, fold)
 
 
 def first_grad_kernel(
@@ -440,30 +436,40 @@
     )(returned, tokens, mask, rep, order_one, order_two, second)
 
 
-def token_grad_kernel(returned_ref, matrix_ref, out_ref):
-    out_ref[...] = mm(returned_ref[...], matrix_ref[...], 0, 0).astype(BF16)
-
-
-def token_gradient(returned, matrix):
-    return pl.pallas_call(
-        token_grad_kernel,
+def outputs_kernel(returned_ref, matrix_two_ref, returned_grad_ref, matrix_one_ref, out_ref, grad_ref):
+    out_ref[...] = mm(returned_ref[...], matrix_two_ref[...], 0, 0).astype(BF16)
+    grad_ref[...] = mm(returned_grad_ref[...], matrix_one_ref[...], 0, 0).astype(BF16)
+
+
+def outputs(returned, matrix_two, returned_grad, matrix_one):
+    return pl.pallas_call(
+        outputs_kernel,
         grid=(WIDE_STEPS,),
-        in_specs=[columns(FEAT, WIDE), whole((FEAT, FEAT))],
-        out_specs=token_rows(),
-        out_shape=struct((TOK, FEAT)),
-        compiler_params=PARAMS,
-        cost_estimate=cost(2 * TOK * FEAT * FEAT, 3 << 20),
-        name="token_gradient",
-    )(returned, matrix)
+        in_specs=[
+            columns(FEAT, WIDE),
+            whole((FEAT, FEAT)),
+            columns(FEAT, WIDE),
+            whole((FEAT, FEAT)),
+        ],
+        out_specs=[token_rows(), token_rows()],
+        out_shape=[struct((TOK, FEAT)), struct((TOK, FEAT))],
+        compiler_params=PARAMS,
+        cost_estimate=cost(4 * TOK * FEAT * FEAT, 7 << 20),
+        name="outputs",
+    )(returned, matrix_two, returned_grad, matrix_one)
 
 
 def exchange(x, bit):
     return lax.ppermute(x, "dp", [(i, i ^ bit) for i in range(PIECES)])
 
 
+def added(one, other):
+    return (one.astype(F32) + other.astype(F32)).astype(BF16)
+
+
 def halved(x, bit):
     rows = x.shape[0] // 2
-    return (x[:rows].astype(F32) + exchange(x[rows:], bit).astype(F32)).astype(BF16)
+    return added(x[:rows], exchange(x[rows:], bit))
 
 
 def to_tensor(x):
@@ -503,13 +509,13 @@
     mixed, act, slope, leaving = mix_forward(arrived, perm, right_one, right_two)
     leaving, arrived_grad = tie((leaving, arrived_grad))
     returned = to_tensor(leaving)
-    leaving_grad, right_shares = mix_backward(
+    leaving_grad, kept, sent = mix_backward(
         me, arrived_grad, perm, right_one, right_two, mixed, act, slope, owner
     )
-    right_shares = halved(right_shares, DP_ORDER[3])
+    right_shares = added(kept, exchange(sent, DP_ORDER[3]))
     returned, leaving_grad, right_shares = tie((returned, leaving_grad, right_shares))
     returned_grad = to_tensor(leaving_grad)
-    output, grad_left_two = output_and_grad(returned, matrix_two, cotangent, mask, fold)
+    grad_left_two = second_grad(returned, cotangent, mask, fold)
     right_shares, grad_left_two = tie((right_shares, grad_left_two))
     right_shares = halved(right_shares, DP_ORDER[2])
     right_shares = halved(right_shares, DP_ORDER[1])
@@ -518,8 +524,8 @@
         returned_grad, tokens, mask, rep, place_one, place_two, grad_left_two
     )
     left_shares = lax.all_to_all(left_held, "dp", split_axis=0, concat_axis=0, tiled=True)
-    returned_grad, left_held = tie((returned_grad, left_held))
-    token_grad = token_gradient(returned_grad, matrix_one)
+    returned_grad, right_shares, left_held = tie((returned_grad, right_shares, left_held))
+    output, token_grad = outputs(returned, matrix_two, returned_grad, matrix_one)
 
     right_total = halved(right_shares, DP_ORDER[0]).astype(F32)
 

time: 178 us -> 170 us (0.955)
  waiting for transfers between devices: 61.3 us -> 56.5 us
  Pallas kernels: 65.6 us -> 63.1 us
  starting transfers between devices: 40.5 us -> 42.6 us
  local copies, waits for them, and re-layouts: 6.21 us -> 4.43 us
    ppermute x4, waiting for transfers between devices: 24.9 us -> 20.2 us  [exchange(): return lax.ppermute(x, 'dp', [(i, i ^ bit) for i in range(PIECES)])]
    all_to_all x1, waiting for transfers between devices: 6.84 us -> 3.58 us  [local(): lax.all_to_all(left_held, 'dp', split_axis=0, concat_axis=0, tiled=True)]
    all_to_all x4, waiting for transfers between devices: 17.6 us -> 20.6 us  [to_tensor(): return lax.all_to_all(x, 'tensor', split_axis=0, concat_axis=0, tiled=True)]
    ppermute x4, starting transfers between devices: 3.49 us -> 6.13 us  [exchange(): return lax.ppermute(x, 'dp', [(i, i ^ bit) for i in range(PIECES)])]
  transfers between devices with their start and end apart: 10 -> 10, of which waited for: 8 -> 8; matrix products, arithmetic and copies ran while one was open for 2% -> 1% of each run, Pallas kernels for 32% -> 32%
where the time goes in v3:
time: 170 us; the launch traced here: 169 us
  Pallas kernels  63.1 us (37%)
  waiting for transfers between devices  56.5 us (33%)
  starting transfers between devices  42.6 us (25%)
  local copies, waits for them, and re-layouts  4.43 us (3%)
  other arithmetic  1.81 us (1%)
    all_to_all x4, starting transfers between devices, to_tensor(): return lax.all_to_all(x, 'tensor', split_axis=0, concat_axis=0, tiled=True)  22.8 us
    all_to_all x4, waiting for transfers between devices, to_tensor(): return lax.all_to_all(x, 'tensor', split_axis=0, concat_axis=0, tiled=True)  20.6 us
    ppermute x4, waiting for transfers between devices, exchange(): return lax.ppermute(x, 'dp', [(i, i ^ bit) for i in range(PIECES)])  20.2 us
    pallas_call x1, Pallas kernels, mix_forward(): pl.pallas_call(forward_kernel, grid=(STEPS,), in_specs=[columns(FEAT), wh...  16.3 us
    pallas_call x1, Pallas kernels, mix_backward(): pl.pallas_call(backward_kernel, grid=(STEPS,), in_specs=[pl.BlockSpec(mem...  14.6 us
    all_to_all x1, waiting for transfers between devices, local(): lax.all_to_all(pieces, 'dp', split_axis=0, concat_axis=0, tiled=True)  12.1 us
    all_to_all x1, starting transfers between devices, local(): lax.all_to_all(pieces, 'dp', split_axis=0, concat_axis=0, tiled=True)  10.2 us
    pallas_call x2, Pallas kernels, block_map(): pl.pallas_call(kernel, grid=(WIDE_STEPS,), in_specs=[token_rows(), piece_...  8.4 us
  transfers between devices with their start and end apart: 10, of which 8 were waited for; matrix products, arithmetic and copies ran while one was open for 1% of the time, Pallas kernels for 32%

profile of v3, /device:TPU:2, one launch (start us, length us, event | category | flops | bytes accessed | tf_op | source)
XLA Modules:
  0.0 169.2 jit_solution(16753556150014758880)
XLA Ops:
  0.6 0.7 reshape.55
  1.4 0.8 copy.14
  2.1 0.1 reshape.54
  2.2 0.7 pad_maximum_fusion.1
  2.9 0.9 broadcast_in_dim.12
  3.8 10.2 %all-to-all-start = ((bf16[16,144,128]{2,1,0:T(8,128)(2,1)}), bf16[16,144,128]{2,1,0:T(8,128)(2,1)}, u32[]{:S(2)}, u32[]{:S(2)}) async-start(bf16[16,144,128]{2,1,0:T(8,128)(2,1)} %broadcast_in_dim.12), calls=%async_computation | async-start | bytes 1179648 | tf_op jit(solution)/shard_map/all_to_all | solution.py:491
  14.0 8.3 %prepare.1 = (bf16[2048,384]{1,0:T(8,128)(2,1)}, bf16[768,384]{1,0:T(8,128)(2,1)}, bf16[768,384]{1,0:T(8,128)(2,1)}, bf16[768,768]{1,0:T(8,128)(2,1)}, bf16[384,...) custom-call(s32[1,64]{1,0:T(1,128)} %bitcast.41, ...), custom_call_target="tpu_custom_call" | custom-call | flops 402653184 | bytes 12582912 | tf_op jit(solution)/shard_map/prepare/pallas_call | solution.py:144
  22.3 12.1 %all-to-all-done.pieces_ref.two_ref.one_ref = bf16[16,144,128]{2,1,0:T(8,128)(2,1)} async-done(((bf16[16,144,128]{2,1,0:T(8,128)(2,1)}), bf16[16,144,128]{2,1,0:T(8,128)(2,1)}, u32[]{:S(2)}, u32[]{:S(2)}) %all-to-all-start) | async-done | bytes 589856 | tf_op jit(solution)/shard_map/all_to_all | solution.py:491
  34.4 4.1 %first_map.1 = (bf16[384,384]{1,0:T(8,128)(2,1)}, bf16[384,2048]{1,0:T(8,128)(2,1)}) custom-call(bf16[2048,384]{1,0:T(8,128)(2,1)} %get-tuple-element.45.tokens_ref, bf16[16,144,128]{2,1,0:T(8,128)(2,1)} %all-to-all-done.pieces_ref.two_ref.one_ref, bf16[768,384]{1,0:T(8,128)(2,1)} %get-tuple-element.47.place_ref.order_one_ref, ...), custom_call_target="tpu_custom_call" | custom-call | flops 1811939328 | bytes 5242880 | tf_op jit(solution)/shard_map/first_map/pallas_call | solution.py:182
  38.5 5.9 %all-to-all-start.1 = ((bf16[16,24,2048]{2,1,0:T(8,128)(2,1)}), bf16[16,24,2048]{2,1,0:T(8,128)(2,1)}, u32[]{:S(2)}, u32[]{:S(2)}) async-start(bf16[16,24,2048]{2,1,0:T(8,128)(2,1)} %bitcast.31), calls=%async_computation.1 | async-start | bytes 3145728 | tf_op jit(solution)/shard_map/all_to_all | solution.py:476
  44.4 2.8 %arrange.1 = (bf16[6,64,256]{2,1,0:T(8,128)(2,1)}, bf16[6,256,64]{2,1,0:T(8,128)(2,1)}) custom-call(bf16[16,144,128]{2,1,0:T(8,128)(2,1)} %all-to-all-done.pieces_ref.two_ref.one_ref, bf16[16,144,128]{2,1,0:T(8,128)(2,1)} %all-to-all-done.pieces_ref.two_ref.one_ref, bf16[768,768]{1,0:T(8,128)(2,1)} %get-tuple-element.54.owner_ref), custom_call_target="tpu_custom_call" | custom-call | flops 150994944 | bytes 3145728 | tf_op jit(solution)/shard_map/arrange/pallas_call | solution.py:213
  47.3 4.3 %second_map_back.1 = (bf16[384,384]{1,0:T(8,128)(2,1)}, bf16[384,2048]{1,0:T(8,128)(2,1)}) custom-call(bf16[2048,384]{1,0:T(8,128)(2,1)} %upstream_ref.3, bf16[16,144,128]{2,1,0:T(8,128)(2,1)} %all-to-all-done.pieces_ref.two_ref.one_ref, bf16[768,384]{1,0:T(8,128)(2,1)} %get-tuple-element.51.place_ref.order_two_ref, ...), custom_call_target="tpu_custom_call" | custom-call | flops 1811939328 | bytes 5242880 | tf_op jit(solution)/shard_map/second_map_back/pallas_call | solution.py:182
  51.5 14.0 %all-to-all-done.1 = bf16[16,24,2048]{2,1,0:T(8,128)(2,1)} async-done(((bf16[16,24,2048]{2,1,0:T(8,128)(2,1)}), bf16[16,24,2048]{2,1,0:T(8,128)(2,1)}, u32[]{:S(2)}, u32[]{:S(2)}) %all-to-all-start.1) | async-done | bytes 1572896 | tf_op jit(solution)/shard_map/all_to_all | solution.py:476
  65.6 5.5 %all-to-all-start.2 = ((bf16[16,24,2048]{2,1,0:T(8,128)(2,1)}), bf16[16,24,2048]{2,1,0:T(8,128)(2,1)}, u32[]{:S(2)}, u32[]{:S(2)}) async-start(bf16[16,24,2048]{2,1,0:T(8,128)(2,1)} %bitcast.30), calls=%async_computation.2 | async-start | bytes 3145728 | tf_op jit(solution)/shard_map/all_to_all | solution.py:476
  71.0 16.3 %mix_forward.1 = (bf16[384,2048]{1,0:T(8,128)(2,1)}, bf16[1536,2048]{1,0:T(8,128)(2,1)}, bf16[1536,2048]{1,0:T(8,128)(2,1)}, bf16[384,2048]{1,0:T(8,128)(2,1)}) custom-call(bf16[384,2048]{1,0:T(8,128)(2,1)} %bitcast.8.arrived_ref, bf16[384,384]{1,0:T(8,128)(2,1)} %get-tuple-element.57.perm_ref, bf16[6,64,256]{2,1,0:T(8,128)(2,1)} %get-tuple-element.58.right_one_ref, ...), custom_call_target="tpu_custom_call" | custom-call | flops 3623878656 | bytes 17825792 | tf_op jit(solution)/shard_map/mix_forward/pallas_call | solution.py:247
  87.4 4.8 %all-to-all-done.2 = bf16[16,24,2048]{2,1,0:T(8,128)(2,1)} async-done(((bf16[16,24,2048]{2,1,0:T(8,128)(2,1)}), bf16[16,24,2048]{2,1,0:T(8,128)(2,1)}, u32[]{:S(2)}, u32[]{:S(2)}) %all-to-all-start.2) | async-done | bytes 1572896 | tf_op jit(solution)/shard_map/all_to_all | solution.py:476
  92.2 5.5 %all-to-all-start.3 = ((bf16[16,24,2048]{2,1,0:T(8,128)(2,1)}), bf16[16,24,2048]{2,1,0:T(8,128)(2,1)}, u32[]{:S(2)}, u32[]{:S(2)}) async-start(bf16[16,24,2048]{2,1,0:T(8,128)(2,1)} %bitcast.29), calls=%async_computation.3 | async-start | bytes 3145728 | tf_op jit(solution)/shard_map/all_to_all | solution.py:476
  97.7 14.6 %mix_backward.1 = (bf16[384,2048]{1,0:T(8,128)(2,1)}, bf16[768,128]{1,0:T(8,128)(2,1)}, bf16[768,128]{1,0:T(8,128)(2,1)}) custom-call(s32[1]{0:T(128)} %bitcast.13.me_ref, bf16[384,2048]{1,0:T(8,128)(2,1)} %bitcast.10.arrived_ref, bf16[384,384]{1,0:T(8,128)(2,1)} %get-tuple-element.57.perm_ref, bf16[6,64,256]{2,1,0:T(8,128)(2,1)} %get-tuple-element.58.right_one_ref, ...), custom_call_target="tpu_custom_call" | custom-call | flops 6039797760 | bytes 17825792 | tf_op jit(solution)/shard_map/mix_backward/pallas_call | solution.py:331
  112.3 0.1 collective-permute-start
  112.4 7.2 %collective-permute-done = bf16[768,128]{1,0:T(8,128)(2,1)S(1)} collective-permute-done((bf16[768,128]{1,0:T(8,128)(2,1)}, bf16[768,128]{1,0:T(8,128)(2,1)S(1)}, u32[]{:S(2)}, u32[]{:S(2)}) %collective-permute-start) | collective-permute-done | bytes 196640 | tf_op jit(solution)/shard_map/ppermute | solution.py:463
  119.6 1.0 add_convert_fusion
  120.6 0.0 all-to-all-done.3
  120.6 5.8 %all-to-all-start.4 = ((bf16[16,24,2048]{2,1,0:T(8,128)(2,1)}), bf16[16,24,2048]{2,1,0:T(8,128)(2,1)}, u32[]{:S(2)}, u32[]{:S(2)}) async-start(bf16[16,24,2048]{2,1,0:T(8,128)(2,1)} %bitcast.28), calls=%async_computation.4 | async-start | bytes 3145728 | tf_op jit(solution)/shard_map/all_to_all | solution.py:476
  126.4 3.6 %second_grad.1.second_ref = bf16[384,128]{1,0:T(8,128)(2,1)} custom-call(bf16[384,2048]{1,0:T(8,128)(2,1)} %bitcast.12.returned_ref, bf16[2048,384]{1,0:T(8,128)(2,1)} %upstream_ref.3, bf16[384,384]{1,0:T(8,128)(2,1)} %get-tuple-element.49.mask_ref, bf16[384,128]{1,0:T(8,128)(2,1)} %get-tuple-element.74.fold_ref), custom_call_target="tpu_custom_call" | custom-call | flops 603979776 | bytes 4194304 | tf_op jit(solution)/shard_map/second_grad/pallas_call | solution.py:377
  130.0 0.8 collective-permute-start.1
  130.8 6.9 %collective-permute-done.1 = bf16[384,128]{1,0:T(8,128)(2,1)S(1)} collective-permute-done((bf16[384,128]{1,0:T(8,128)(2,1)S(1)}, bf16[384,128]{1,0:T(8,128)(2,1)S(1)}, u32[]{:S(2)}, u32[]{:S(2)}) %collective-permute-start.1) | collective-permute-done | bytes 98336 | tf_op jit(solution)/shard_map/ppermute | solution.py:463
  137.7 1.9 %collective-permute-start.2 = (bf16[192,128]{1,0:T(8,128)(2,1)S(1)}, bf16[192,128]{1,0:T(8,128)(2,1)S(1)}, u32[]{:S(2)}, u32[]{:S(2)}) collective-permute-start(bf16[192,128]{1,0:T(8,128)(2,1)S(1)} %slice.59), channel_id=1, source_target_pairs={{0,128},{16,144},{32,160},{48,176},{64,192},{80,208},{96,224},{112... | collective-permute-start | bytes 147464 | tf_op jit(solution)/shard_map/ppermute | solution.py:463
  139.5 6.2 %collective-permute-done.2 = bf16[192,128]{1,0:T(8,128)(2,1)S(1)} collective-permute-done((bf16[192,128]{1,0:T(8,128)(2,1)S(1)}, bf16[192,128]{1,0:T(8,128)(2,1)S(1)}, u32[]{:S(2)}, u32[]{:S(2)}) %collective-permute-start.2) | collective-permute-done | bytes 49184 | tf_op jit(solution)/shard_map/ppermute | solution.py:463
  145.8 1.7 %all-to-all-done.4 = bf16[16,24,2048]{2,1,0:T(8,128)(2,1)} async-done(((bf16[16,24,2048]{2,1,0:T(8,128)(2,1)}), bf16[16,24,2048]{2,1,0:T(8,128)(2,1)}, u32[]{:S(2)}, u32[]{:S(2)}) %all-to-all-start.4) | async-done | bytes 1572896 | tf_op jit(solution)/shard_map/all_to_all | solution.py:476
  147.5 4.3 %first_grad.1 = bf16[768,128]{1,0:T(8,128)(2,1)} custom-call(bf16[384,2048]{1,0:T(8,128)(2,1)} %bitcast.15.returned_ref.returned_grad_ref, bf16[2048,384]{1,0:T(8,128)(2,1)} %get-tuple-element.45.tokens_ref, bf16[384,384]{1,0:T(8,128)(2,1)} %get-tuple-element.49.mask_ref, bf16[384,128]{1,0:T(8,128)(2,1)} %get-tuple-element.48.rep_ref, ...), custom_call_target="tpu_custom_call" | custom-call | flops 603979776 | bytes 3145728 | tf_op jit(solution)/shard_map/first_grad/pallas_call | solution.py:418
  151.8 3.5 %all-to-all-start.5 = ((bf16[16,48,128]{2,1,0:T(8,128)(2,1)}), bf16[16,48,128]{2,1,0:T(8,128)(2,1)S(1)}, u32[]{:S(2)}, u32[]{:S(2)}) async-start(bf16[16,48,128]{2,1,0:T(8,128)(2,1)} %bitcast.32), calls=%async_computation.5 | async-start | bytes 393216 | tf_op jit(solution)/shard_map/all_to_all | solution.py:526
  155.4 3.4 %collective-permute-start.3 = (bf16[96,128]{1,0:T(8,128)(2,1)S(1)}, bf16[96,128]{1,0:T(8,128)(2,1)S(1)}, u32[]{:S(2)}, u32[]{:S(2)}) collective-permute-start(bf16[96,128]{1,0:T(8,128)(2,1)S(1)} %slice.51), channel_id=1, source_target_pairs={{0,16},{16,0},{32,48},{48,32},{64,80},{80,64},{96,112},{112,96},{1... | collective-permute-start | bytes 73736 | tf_op jit(solution)/shard_map/ppermute | solution.py:463
  158.8 4.8 %outputs.1 = (bf16[2048,384]{1,0:T(8,128)(2,1)}, bf16[2048,384]{1,0:T(8,128)(2,1)}) custom-call(bf16[384,2048]{1,0:T(8,128)(2,1)} %bitcast.12.returned_ref, bf16[384,384]{1,0:T(8,128)(2,1)} %get-tuple-element.71.matrix_two_ref, bf16[384,2048]{1,0:T(8,128)(2,1)} %bitcast.15.returned_ref.returned_grad_ref, bf16[384,384]{1,0:T(8,128)(2,1)} %get-tuple-element.78.matrix_one_ref), custom_call_target="tpu_custom_call" | custom-call | flops 1207959552 | bytes 7340032 | tf_op jit(solution)/shard_map/outputs/pallas_call | solution.py:445
  163.5 0.0 collective-permute-done.3
  163.6 0.6 reshape.58
  164.2 0.1 reshape.59
  164.3 0.6 copy.15
  164.9 3.6 %all-to-all-done.5 = bf16[16,48,128]{2,1,0:T(8,128)(2,1)S(1)} async-done(((bf16[16,48,128]{2,1,0:T(8,128)(2,1)}), bf16[16,48,128]{2,1,0:T(8,128)(2,1)S(1)}, u32[]{:S(2)}, u32[]{:S(2)}) %all-to-all-start.5) | async-done | bytes 196640 | tf_op jit(solution)/shard_map/all_to_all | solution.py:526
  168.5 0.6 slice_bitcast_fusion
  (12 shorter events, 0.1 us)
Async XLA Ops:
  3.8 30.5 %all-to-all-start = ((bf16[16,144,128]{2,1,0:T(8,128)(2,1)}), bf16[16,144,128]{2,1,0:T(8,128)(2,1)}, u32[]{:S(2)}, u32[]{:S(2)}) async-start(bf16[16,144,128]{2,1,0:T(8,128)(2,1)} %broadcast_in_dim.12), calls=%async_computation | async-start | bytes 1179648 | tf_op jit(solution)/shard_map/all_to_all | solution.py:491
  38.5 27.1 %all-to-all-start.1 = ((bf16[16,24,2048]{2,1,0:T(8,128)(2,1)}), bf16[16,24,2048]{2,1,0:T(8,128)(2,1)}, u32[]{:S(2)}, u32[]{:S(2)}) async-start(bf16[16,24,2048]{2,1,0:T(8,128)(2,1)} %bitcast.31), calls=%async_computation.1 | async-start | bytes 3145728 | tf_op jit(solution)/shard_map/all_to_all | solution.py:476
  65.6 26.6 %all-to-all-start.2 = ((bf16[16,24,2048]{2,1,0:T(8,128)(2,1)}), bf16[16,24,2048]{2,1,0:T(8,128)(2,1)}, u32[]{:S(2)}, u32[]{:S(2)}) async-start(bf16[16,24,2048]{2,1,0:T(8,128)(2,1)} %bitcast.30), calls=%async_computation.2 | async-start | bytes 3145728 | tf_op jit(solution)/shard_map/all_to_all | solution.py:476
  92.2 28.4 %all-to-all-start.3 = ((bf16[16,24,2048]{2,1,0:T(8,128)(2,1)}), bf16[16,24,2048]{2,1,0:T(8,128)(2,1)}, u32[]{:S(2)}, u32[]{:S(2)}) async-start(bf16[16,24,2048]{2,1,0:T(8,128)(2,1)} %bitcast.29), calls=%async_computation.3 | async-start | bytes 3145728 | tf_op jit(solution)/shard_map/all_to_all | solution.py:476
  112.3 7.3 %collective-permute-start = (bf16[768,128]{1,0:T(8,128)(2,1)}, bf16[768,128]{1,0:T(8,128)(2,1)S(1)}, u32[]{:S(2)}, u32[]{:S(2)}) collective-permute-start(bf16[768,128]{1,0:T(8,128)(2,1)} %get-tuple-element.69), channel_id=1, source_target_pairs={{0,32},{16,48},{32,0},{48,16},{64,96},{80,112},{96,64},{112,80},{1... | collective-permute-start | bytes 589832 | tf_op jit(solution)/shard_map/ppermute | solution.py:463
  120.6 26.9 %all-to-all-start.4 = ((bf16[16,24,2048]{2,1,0:T(8,128)(2,1)}), bf16[16,24,2048]{2,1,0:T(8,128)(2,1)}, u32[]{:S(2)}, u32[]{:S(2)}) async-start(bf16[16,24,2048]{2,1,0:T(8,128)(2,1)} %bitcast.28), calls=%async_computation.4 | async-start | bytes 3145728 | tf_op jit(solution)/shard_map/all_to_all | solution.py:476
  130.0 7.7 %collective-permute-start.1 = (bf16[384,128]{1,0:T(8,128)(2,1)S(1)}, bf16[384,128]{1,0:T(8,128)(2,1)S(1)}, u32[]{:S(2)}, u32[]{:S(2)}) collective-permute-start(bf16[384,128]{1,0:T(8,128)(2,1)S(1)} %slice.45), channel_id=1, source_target_pairs={{0,64},{16,80},{32,96},{48,112},{64,0},{80,16},{96,32},{112,48},{1... | collective-permute-start | bytes 294920 | tf_op jit(solution)/shard_map/ppermute | solution.py:463
  137.7 8.1 %collective-permute-start.2 = (bf16[192,128]{1,0:T(8,128)(2,1)S(1)}, bf16[192,128]{1,0:T(8,128)(2,1)S(1)}, u32[]{:S(2)}, u32[]{:S(2)}) collective-permute-start(bf16[192,128]{1,0:T(8,128)(2,1)S(1)} %slice.59), channel_id=1, source_target_pairs={{0,128},{16,144},{32,160},{48,176},{64,192},{80,208},{96,224},{112... | collective-permute-start | bytes 147464 | tf_op jit(solution)/shard_map/ppermute | solution.py:463
  151.8 16.7 %all-to-all-start.5 = ((bf16[16,48,128]{2,1,0:T(8,128)(2,1)}), bf16[16,48,128]{2,1,0:T(8,128)(2,1)S(1)}, u32[]{:S(2)}, u32[]{:S(2)}) async-start(bf16[16,48,128]{2,1,0:T(8,128)(2,1)} %bitcast.32), calls=%async_computation.5 | async-start | bytes 393216 | tf_op jit(solution)/shard_map/all_to_all | solution.py:526
  155.4 8.2 %collective-permute-start.3 = (bf16[96,128]{1,0:T(8,128)(2,1)S(1)}, bf16[96,128]{1,0:T(8,128)(2,1)S(1)}, u32[]{:S(2)}, u32[]{:S(2)}) collective-permute-start(bf16[96,128]{1,0:T(8,128)(2,1)S(1)} %slice.51), channel_id=1, source_target_pairs={{0,16},{16,0},{32,48},{48,32},{64,80},{80,64},{96,112},{112,96},{1... | collective-permute-start | bytes 73736 | tf_op jit(solution)/shard_map/ppermute | solution.py:463

commit v4 on v3

--- a/solution.py
+++ b/solution.py
@@ -57,6 +57,34 @@
 
 def offset(place):
     return sum(((place >> level) & 1) * bit for level, bit in enumerate(DP_ORDER))
+
+
+def pack_kernel(left_one_ref, left_two_ref, right_one_ref, right_two_ref, pieces_ref):
+    left = [ref[row].astype(F32) for ref in (left_one_ref, left_two_ref) for row in range(6)]
+    left = jnp.concatenate(left, axis=0)
+    left = jnp.concatenate([left, jnp.zeros((48, 128 - BS), F32)], axis=1)
+    two = [
+        jnp.concatenate([right_two_ref[pos], right_two_ref[pos + POS // 2]], axis=1).astype(F32)
+        for pos in range(POS // 2)
+    ]
+    one = [right_one_ref[pos].astype(F32) for pos in range(POS)]
+    one = [rows[:, half : half + 128] for half in (0, 128) for rows in one]
+    piece = jnp.concatenate([left] + two + one, axis=0).astype(BF16)
+    for place in range(PIECES):
+        pieces_ref[place] = piece
+
+
+def pack(left_one, left_two, right_one, right_two):
+    vmem = pl.BlockSpec(memory_space=pltpu.VMEM)
+    return pl.pallas_call(
+        pack_kernel,
+        in_specs=[vmem] * 4,
+        out_specs=vmem,
+        out_shape=struct((PIECES, 144, 128)),
+        compiler_params=PARAMS,
+        cost_estimate=cost(1 << 20, 1 << 20),
+        name="pack",
+    )(left_one, left_two, right_one, right_two)
 
 
 def prepare_kernel(
@@ -358,7 +386,9 @@
     )(me, arrived, perm, right_one, right_two, mixed, act, slope, owner)
 
 
-def second_grad_kernel(returned_ref, upstream_ref, mask_ref, fold_ref, grad_ref, sum_ref):
+def second_grad_kernel(
+    returned_ref, upstream_ref, mask_ref, fold_ref, order_ref, shares_ref, sum_ref
+):
     step = pl.program_id(0)
 
     @pl.when(step == 0)
@@ -370,21 +400,28 @@
     @pl.when(step == WIDE_STEPS - 1)
     def _():
         kept = sum_ref[...].astype(BF16) * mask_ref[...]
-        grad_ref[...] = mm(kept, fold_ref[...]).astype(BF16)
-
-
-def second_grad(returned, upstream, mask, fold):
+        flat = mm(kept, fold_ref[...]).astype(BF16)
+        shares_ref[...] = mm(order_ref[...], flat).astype(BF16)
+
+
+def second_grad(returned, upstream, mask, fold, order):
     return pl.pallas_call(
         second_grad_kernel,
         grid=(WIDE_STEPS,),
-        in_specs=[columns(FEAT, WIDE), token_rows(), whole((FEAT, FEAT)), whole((FEAT, 128))],
-        out_specs=whole((FEAT, 128)),
-        out_shape=struct((FEAT, 128)),
+        in_specs=[
+            columns(FEAT, WIDE),
+            token_rows(),
+            whole((FEAT, FEAT)),
+            whole((FEAT, 128)),
+            whole((ALL_ROWS, FEAT)),
+        ],
+        out_specs=whole((ALL_ROWS, 128)),
+        out_shape=struct((ALL_ROWS, 128)),
         scratch_shapes=[pltpu.VMEM((FEAT, FEAT), F32)],
         compiler_params=PARAMS,
         cost_estimate=cost(2 * TOK * FEAT * FEAT, 4 << 20),
         name="second_grad",
-    )(returned, upstream, mask, fold)
+    )(returned, upstream, mask, fold, order)
 
 
 def first_grad_kernel(
@@ -392,8 +429,7 @@
     tokens_ref,
     mask_ref,
     rep_ref,
-    order_one_ref,
-    order_two_ref,
+    order_ref,
     second_ref,
     shares_ref,
     sum_ref,
@@ -410,11 +446,10 @@
     def _():
         kept = sum_ref[...].astype(BF16) * mask_ref[...]
         flat = mm(rep_ref[...], kept, 0, 0).astype(BF16)
-        shares = mm(order_one_ref[...], flat, 1, 1) + mm(order_two_ref[...], second_ref[...])
-        shares_ref[...] = shares.astype(BF16)
-
-
-def first_grad(returned, tokens, mask, rep, order_one, order_two, second):
+        shares_ref[...] = (mm(order_ref[...], flat, 1, 1) + second_ref[...].astype(F32)).astype(BF16)
+
+
+def first_grad(returned, tokens, mask, rep, order, second):
     return pl.pallas_call(
         first_grad_kernel,
         grid=(WIDE_STEPS,),
@@ -424,8 +459,7 @@
             whole((FEAT, FEAT)),
             whole((FEAT, 128)),
             whole((ALL_ROWS, FEAT)),
-            whole((ALL_ROWS, FEAT)),
-            whole((FEAT, 128)),
+            whole((ALL_ROWS, 128)),
         ],
         out_specs=whole((ALL_ROWS, 128)),
         out_shape=struct((ALL_ROWS, 128)),
@@ -433,7 +467,7 @@
         compiler_params=PARAMS,
         cost_estimate=cost(2 * TOK * FEAT * FEAT, 3 << 20),
         name="first_grad",
-    )(returned, tokens, mask, rep, order_one, order_two, second)
+    )(returned, tokens, mask, rep, order, second)
 
 
 def outputs_kernel(returned_ref, matrix_two_ref, returned_grad_ref, matrix_one_ref, out_ref, grad_ref):
@@ -482,12 +516,9 @@
     tie = lax.optimization_barrier
     me = lax.axis_index("dp").astype(jnp.int32).reshape(1)
 
-    left = jnp.concatenate([first_left.transpose(1, 0, 2), second_left.transpose(1, 0, 2)], axis=0)
-    left = jnp.pad(left.reshape(48, BS), ((0, 0), (0, 128 - BS)))
-    two = second_right.reshape(2, 3, 16, NB).transpose(1, 2, 0, 3).reshape(48, 128)
-    one = first_right.reshape(24, HB)
-    piece = jnp.concatenate([left, two, one[:, :128], one[:, 128:]], axis=0)
-    pieces = jnp.broadcast_to(piece[None], (PIECES, 144, 128))
+    pieces = pack(
+        first_left.transpose(1, 0, 2), second_left.transpose(1, 0, 2), first_right, second_right
+    )
     pieces = lax.all_to_all(pieces, "dp", split_axis=0, concat_axis=0, tiled=True)
 
     tokens, place_one, place_two, owner, perm, mask, rep, fold, spread = prepare(
@@ -515,13 +546,13 @@
     right_shares = added(kept, exchange(sent, DP_ORDER[3]))
     returned, leaving_grad, right_shares = tie((returned, leaving_grad, right_shares))
     returned_grad = to_tensor(leaving_grad)
-    grad_left_two = second_grad(returned, cotangent, mask, fold)
+    grad_left_two = second_grad(returned, cotangent, mask, fold, place_two)
     right_shares, grad_left_two = tie((right_shares, grad_left_two))
     right_shares = halved(right_shares, DP_ORDER[2])
     right_shares = halved(right_shares, DP_ORDER[1])
 
     left_held = first_grad(
-        returned_grad, tokens, mask, rep, place_one, place_two, grad_left_two
+        returned_grad, tokens, mask, rep, place_one, grad_left_two
     )
     left_shares = lax.all_to_all(left_held, "dp", split_axis=0, concat_axis=0, tiled=True)
     returned_grad, right_shares, left_held = tie((returned_grad, right_shares, left_held))

time: 170 us -> 168 us (0.988)
  local copies, waits for them, and re-layouts: 4.43 us -> 1.97 us
  Pallas kernels: 63.1 us -> 65.2 us
  transfers between devices with their start and end apart: 10 -> 10, of which waited for: 8 -> 8; matrix products, arithmetic and copies ran while one was open for 1% -> 1% of each run, Pallas kernels for 32% -> 33%
where the time goes in v4:
time: 168 us; the launch traced here: 167 us
  Pallas kernels  65.2 us (39%)
  waiting for transfers between devices  55.9 us (33%)
  starting transfers between devices  42.6 us (25%)
  local copies, waits for them, and re-layouts  1.97 us (1%)
    all_to_all x4, starting transfers between devices, to_tensor(): return lax.all_to_all(x, 'tensor', split_axis=0, concat_axis=0, tiled=True)  22.8 us
    ppermute x4, waiting for transfers between devices, exchange(): return lax.ppermute(x, 'dp', [(i, i ^ bit) for i in range(PIECES)])  20.2 us
    all_to_all x4, waiting for transfers between devices, to_tensor(): return lax.all_to_all(x, 'tensor', split_axis=0, concat_axis=0, tiled=True)  20 us
    pallas_call x1, Pallas kernels, mix_forward(): pl.pallas_call(forward_kernel, grid=(STEPS,), in_specs=[columns(FEAT), wh...  16.3 us
    pallas_call x1, Pallas kernels, mix_backward(): pl.pallas_call(backward_kernel, grid=(STEPS,), in_specs=[pl.BlockSpec(mem...  14.6 us
    all_to_all x1, waiting for transfers between devices, local(): lax.all_to_all(pieces, 'dp', split_axis=0, concat_axis=0, tiled=True)  12.1 us
    all_to_all x1, starting transfers between devices, local(): lax.all_to_all(pieces, 'dp', split_axis=0, concat_axis=0, tiled=True)  10.2 us
    pallas_call x2, Pallas kernels, block_map(): pl.pallas_call(kernel, grid=(WIDE_STEPS,), in_specs=[token_rows(), piece_...  8.38 us
  transfers between devices with their start and end apart: 10, of which 8 were waited for; matrix products, arithmetic and copies ran while one was open for 1% of the time, Pallas kernels for 33%

profile of v4, /device:TPU:2, one launch (start us, length us, event | category | flops | bytes accessed | tf_op | source)
XLA Modules:
  0.0 167.4 jit_solution(5091241621582654360)
XLA Ops:
  0.6 1.7 %pack.1 = bf16[16,144,128]{2,1,0:T(8,128)(2,1)} custom-call(bf16[6,4,96]{2,1,0:T(4,128)(2,1)} %bitcast.33, bf16[6,4,96]{2,1,0:T(4,128)(2,1)} %bitcast.34, bf16[6,4,256]{2,1,0:T(4,128)(2,1)} %right_one_ref.1, bf16[6,16,64]{2,1,0:T(8,128)(2,1)} %right_two_ref.1), custom_call_target="tpu_custom_call" | custom-call | flops 1048576 | bytes 1048576 | tf_op jit(solution)/shard_map/pack/pallas_call | solution.py:79
  2.3 10.2 %all-to-all-start = ((bf16[16,144,128]{2,1,0:T(8,128)(2,1)}), bf16[16,144,128]{2,1,0:T(8,128)(2,1)}, u32[]{:S(2)}, u32[]{:S(2)}) async-start(bf16[16,144,128]{2,1,0:T(8,128)(2,1)} %pack.1), calls=%async_computation | async-start | bytes 1179648 | tf_op jit(solution)/shard_map/all_to_all | solution.py:522
  12.5 8.3 %prepare.1 = (bf16[2048,384]{1,0:T(8,128)(2,1)}, bf16[768,384]{1,0:T(8,128)(2,1)}, bf16[768,384]{1,0:T(8,128)(2,1)}, bf16[768,768]{1,0:T(8,128)(2,1)}, bf16[384,...) custom-call(s32[1,64]{1,0:T(1,128)} %bitcast.35, ...), custom_call_target="tpu_custom_call" | custom-call | flops 402653184 | bytes 12582912 | tf_op jit(solution)/shard_map/prepare/pallas_call | solution.py:172
  20.8 12.1 %all-to-all-done.pieces_ref.two_ref.one_ref = bf16[16,144,128]{2,1,0:T(8,128)(2,1)} async-done(((bf16[16,144,128]{2,1,0:T(8,128)(2,1)}), bf16[16,144,128]{2,1,0:T(8,128)(2,1)}, u32[]{:S(2)}, u32[]{:S(2)}) %all-to-all-start) | async-done | bytes 589856 | tf_op jit(solution)/shard_map/all_to_all | solution.py:522
  32.8 4.1 %first_map.1 = (bf16[384,384]{1,0:T(8,128)(2,1)}, bf16[384,2048]{1,0:T(8,128)(2,1)}) custom-call(bf16[2048,384]{1,0:T(8,128)(2,1)} %get-tuple-element.45.tokens_ref, bf16[16,144,128]{2,1,0:T(8,128)(2,1)} %all-to-all-done.pieces_ref.two_ref.one_ref, bf16[768,384]{1,0:T(8,128)(2,1)} %get-tuple-element.47.place_ref.order_ref, ...), custom_call_target="tpu_custom_call" | custom-call | flops 1811939328 | bytes 5242880 | tf_op jit(solution)/shard_map/first_map/pallas_call | solution.py:210
  37.0 5.9 %all-to-all-start.1 = ((bf16[16,24,2048]{2,1,0:T(8,128)(2,1)}), bf16[16,24,2048]{2,1,0:T(8,128)(2,1)}, u32[]{:S(2)}, u32[]{:S(2)}) async-start(bf16[16,24,2048]{2,1,0:T(8,128)(2,1)} %bitcast.27), calls=%async_computation.1 | async-start | bytes 3145728 | tf_op jit(solution)/shard_map/all_to_all | solution.py:510
  42.9 2.9 %arrange.1 = (bf16[6,64,256]{2,1,0:T(8,128)(2,1)}, bf16[6,256,64]{2,1,0:T(8,128)(2,1)}) custom-call(bf16[16,144,128]{2,1,0:T(8,128)(2,1)} %all-to-all-done.pieces_ref.two_ref.one_ref, bf16[16,144,128]{2,1,0:T(8,128)(2,1)} %all-to-all-done.pieces_ref.two_ref.one_ref, bf16[768,768]{1,0:T(8,128)(2,1)} %get-tuple-element.54.owner_ref), custom_call_target="tpu_custom_call" | custom-call | flops 150994944 | bytes 3145728 | tf_op jit(solution)/shard_map/arrange/pallas_call | solution.py:241
  45.8 4.3 %second_map_back.1 = (bf16[384,384]{1,0:T(8,128)(2,1)}, bf16[384,2048]{1,0:T(8,128)(2,1)}) custom-call(bf16[2048,384]{1,0:T(8,128)(2,1)} %upstream_ref.3, bf16[16,144,128]{2,1,0:T(8,128)(2,1)} %all-to-all-done.pieces_ref.two_ref.one_ref, bf16[768,384]{1,0:T(8,128)(2,1)} %get-tuple-element.51.place_ref.order_ref, ...), custom_call_target="tpu_custom_call" | custom-call | flops 1811939328 | bytes 5242880 | tf_op jit(solution)/shard_map/second_map_back/pallas_call | solution.py:210
  50.0 14.0 %all-to-all-done.1 = bf16[16,24,2048]{2,1,0:T(8,128)(2,1)} async-done(((bf16[16,24,2048]{2,1,0:T(8,128)(2,1)}), bf16[16,24,2048]{2,1,0:T(8,128)(2,1)}, u32[]{:S(2)}, u32[]{:S(2)}) %all-to-all-start.1) | async-done | bytes 1572896 | tf_op jit(solution)/shard_map/all_to_all | solution.py:510
  64.0 5.5 %all-to-all-start.2 = ((bf16[16,24,2048]{2,1,0:T(8,128)(2,1)}), bf16[16,24,2048]{2,1,0:T(8,128)(2,1)}, u32[]{:S(2)}, u32[]{:S(2)}) async-start(bf16[16,24,2048]{2,1,0:T(8,128)(2,1)} %bitcast.26), calls=%async_computation.2 | async-start | bytes 3145728 | tf_op jit(solution)/shard_map/all_to_all | solution.py:510
  69.5 16.3 %mix_forward.1 = (bf16[384,2048]{1,0:T(8,128)(2,1)}, bf16[1536,2048]{1,0:T(8,128)(2,1)}, bf16[1536,2048]{1,0:T(8,128)(2,1)}, bf16[384,2048]{1,0:T(8,128)(2,1)}) custom-call(bf16[384,2048]{1,0:T(8,128)(2,1)} %bitcast.5.arrived_ref, bf16[384,384]{1,0:T(8,128)(2,1)} %get-tuple-element.57.perm_ref, bf16[6,64,256]{2,1,0:T(8,128)(2,1)} %get-tuple-element.58.right_one_ref, ...), custom_call_target="tpu_custom_call" | custom-call | flops 3623878656 | bytes 17825792 | tf_op jit(solution)/shard_map/mix_forward/pallas_call | solution.py:275
  85.9 4.8 %all-to-all-done.2 = bf16[16,24,2048]{2,1,0:T(8,128)(2,1)} async-done(((bf16[16,24,2048]{2,1,0:T(8,128)(2,1)}), bf16[16,24,2048]{2,1,0:T(8,128)(2,1)}, u32[]{:S(2)}, u32[]{:S(2)}) %all-to-all-start.2) | async-done | bytes 1572896 | tf_op jit(solution)/shard_map/all_to_all | solution.py:510
  90.7 5.5 %all-to-all-start.3 = ((bf16[16,24,2048]{2,1,0:T(8,128)(2,1)}), bf16[16,24,2048]{2,1,0:T(8,128)(2,1)}, u32[]{:S(2)}, u32[]{:S(2)}) async-start(bf16[16,24,2048]{2,1,0:T(8,128)(2,1)} %bitcast.25), calls=%async_computation.3 | async-start | bytes 3145728 | tf_op jit(solution)/shard_map/all_to_all | solution.py:510
  96.2 14.6 %mix_backward.1 = (bf16[384,2048]{1,0:T(8,128)(2,1)}, bf16[768,128]{1,0:T(8,128)(2,1)}, bf16[768,128]{1,0:T(8,128)(2,1)}) custom-call(s32[1]{0:T(128)} %bitcast.10.me_ref, bf16[384,2048]{1,0:T(8,128)(2,1)} %bitcast.7.arrived_ref, bf16[384,384]{1,0:T(8,128)(2,1)} %get-tuple-element.57.perm_ref, bf16[6,64,256]{2,1,0:T(8,128)(2,1)} %get-tuple-element.58.right_one_ref, ...), custom_call_target="tpu_custom_call" | custom-call | flops 6039797760 | bytes 17825792 | tf_op jit(solution)/shard_map/mix_backward/pallas_call | solution.py:359
  110.8 0.1 collective-permute-start
  110.9 7.2 %collective-permute-done = bf16[768,128]{1,0:T(8,128)(2,1)S(1)} collective-permute-done((bf16[768,128]{1,0:T(8,128)(2,1)}, bf16[768,128]{1,0:T(8,128)(2,1)S(1)}, u32[]{:S(2)}, u32[]{:S(2)}) %collective-permute-start) | collective-permute-done | bytes 196640 | tf_op jit(solution)/shard_map/ppermute | solution.py:497
  118.1 1.0 add_convert_fusion
  119.0 0.0 all-to-all-done.3
  119.1 5.8 %all-to-all-start.4 = ((bf16[16,24,2048]{2,1,0:T(8,128)(2,1)}), bf16[16,24,2048]{2,1,0:T(8,128)(2,1)}, u32[]{:S(2)}, u32[]{:S(2)}) async-start(bf16[16,24,2048]{2,1,0:T(8,128)(2,1)} %bitcast.24), calls=%async_computation.4 | async-start | bytes 3145728 | tf_op jit(solution)/shard_map/all_to_all | solution.py:510
  124.8 4.2 %second_grad.1.second_ref = bf16[768,128]{1,0:T(8,128)(2,1)} custom-call(bf16[384,2048]{1,0:T(8,128)(2,1)} %bitcast.9.returned_ref, bf16[2048,384]{1,0:T(8,128)(2,1)} %upstream_ref.3, bf16[384,384]{1,0:T(8,128)(2,1)} %get-tuple-element.49.mask_ref, bf16[384,128]{1,0:T(8,128)(2,1)} %get-tuple-element.74.fold_ref, ...), custom_call_target="tpu_custom_call" | custom-call | flops 603979776 | bytes 4194304 | tf_op jit(solution)/shard_map/second_grad/pallas_call | solution.py:408
  129.0 0.8 collective-permute-start.1
  129.8 6.9 %collective-permute-done.1 = bf16[384,128]{1,0:T(8,128)(2,1)S(1)} collective-permute-done((bf16[384,128]{1,0:T(8,128)(2,1)S(1)}, bf16[384,128]{1,0:T(8,128)(2,1)S(1)}, u32[]{:S(2)}, u32[]{:S(2)}) %collective-permute-start.1) | collective-permute-done | bytes 98336 | tf_op jit(solution)/shard_map/ppermute | solution.py:497
  136.7 1.9 %collective-permute-start.2 = (bf16[192,128]{1,0:T(8,128)(2,1)S(1)}, bf16[192,128]{1,0:T(8,128)(2,1)S(1)}, u32[]{:S(2)}, u32[]{:S(2)}) collective-permute-start(bf16[192,128]{1,0:T(8,128)(2,1)S(1)} %slice.49), channel_id=1, source_target_pairs={{0,128},{16,144},{32,160},{48,176},{64,192},{80,208},{96,224},{112... | collective-permute-start | bytes 147464 | tf_op jit(solution)/shard_map/ppermute | solution.py:497
  138.6 6.2 %collective-permute-done.2 = bf16[192,128]{1,0:T(8,128)(2,1)S(1)} collective-permute-done((bf16[192,128]{1,0:T(8,128)(2,1)S(1)}, bf16[192,128]{1,0:T(8,128)(2,1)S(1)}, u32[]{:S(2)}, u32[]{:S(2)}) %collective-permute-start.2) | collective-permute-done | bytes 49184 | tf_op jit(solution)/shard_map/ppermute | solution.py:497
  144.8 1.1 all-to-all-done.4
  146.0 4.1 %first_grad.1 = bf16[768,128]{1,0:T(8,128)(2,1)} custom-call(bf16[384,2048]{1,0:T(8,128)(2,1)} %bitcast.12.returned_ref.returned_grad_ref, bf16[2048,384]{1,0:T(8,128)(2,1)} %get-tuple-element.45.tokens_ref, bf16[384,384]{1,0:T(8,128)(2,1)} %get-tuple-element.49.mask_ref, bf16[384,128]{1,0:T(8,128)(2,1)} %get-tuple-element.48.rep_ref, ...), custom_call_target="tpu_custom_call" | custom-call | flops 603979776 | bytes 3145728 | tf_op jit(solution)/shard_map/first_grad/pallas_call | solution.py:453
  150.1 3.5 %all-to-all-start.5 = ((bf16[16,48,128]{2,1,0:T(8,128)(2,1)}), bf16[16,48,128]{2,1,0:T(8,128)(2,1)S(1)}, u32[]{:S(2)}, u32[]{:S(2)}) async-start(bf16[16,48,128]{2,1,0:T(8,128)(2,1)} %bitcast.28), calls=%async_computation.5 | async-start | bytes 393216 | tf_op jit(solution)/shard_map/all_to_all | solution.py:557
  153.6 3.4 %collective-permute-start.3 = (bf16[96,128]{1,0:T(8,128)(2,1)S(1)}, bf16[96,128]{1,0:T(8,128)(2,1)S(1)}, u32[]{:S(2)}, u32[]{:S(2)}) collective-permute-start(bf16[96,128]{1,0:T(8,128)(2,1)S(1)} %slice.43), channel_id=1, source_target_pairs={{0,16},{16,0},{32,48},{48,32},{64,80},{80,64},{96,112},{112,96},{1... | collective-permute-start | bytes 73736 | tf_op jit(solution)/shard_map/ppermute | solution.py:497
  157.0 4.8 %outputs.1 = (bf16[2048,384]{1,0:T(8,128)(2,1)}, bf16[2048,384]{1,0:T(8,128)(2,1)}) custom-call(bf16[384,2048]{1,0:T(8,128)(2,1)} %bitcast.9.returned_ref, bf16[384,384]{1,0:T(8,128)(2,1)} %get-tuple-element.71.matrix_two_ref, bf16[384,2048]{1,0:T(8,128)(2,1)} %bitcast.12.returned_ref.returned_grad_ref, bf16[384,384]{1,0:T(8,128)(2,1)} %get-tuple-element.78.matrix_one_ref), custom_call_target="tpu_custom_call" | custom-call | flops 1207959552 | bytes 7340032 | tf_op jit(solution)/shard_map/outputs/pallas_call | solution.py:479
  161.8 0.0 collective-permute-done.3
  161.8 0.6 reshape.41
  162.5 0.1 reshape.42
  162.6 0.6 copy.14
  163.2 3.6 %all-to-all-done.5 = bf16[16,48,128]{2,1,0:T(8,128)(2,1)S(1)} async-done(((bf16[16,48,128]{2,1,0:T(8,128)(2,1)}), bf16[16,48,128]{2,1,0:T(8,128)(2,1)S(1)}, u32[]{:S(2)}, u32[]{:S(2)}) %all-to-all-start.5) | async-done | bytes 196640 | tf_op jit(solution)/shard_map/all_to_all | solution.py:557
  166.8 0.6 slice_bitcast_fusion
  (10 shorter events, 0.1 us)
Async XLA Ops:
  2.3 30.5 %all-to-all-start = ((bf16[16,144,128]{2,1,0:T(8,128)(2,1)}), bf16[16,144,128]{2,1,0:T(8,128)(2,1)}, u32[]{:S(2)}, u32[]{:S(2)}) async-start(bf16[16,144,128]{2,1,0:T(8,128)(2,1)} %pack.1), calls=%async_computation | async-start | bytes 1179648 | tf_op jit(solution)/shard_map/all_to_all | solution.py:522
  37.0 27.1 %all-to-all-start.1 = ((bf16[16,24,2048]{2,1,0:T(8,128)(2,1)}), bf16[16,24,2048]{2,1,0:T(8,128)(2,1)}, u32[]{:S(2)}, u32[]{:S(2)}) async-start(bf16[16,24,2048]{2,1,0:T(8,128)(2,1)} %bitcast.27), calls=%async_computation.1 | async-start | bytes 3145728 | tf_op jit(solution)/shard_map/all_to_all | solution.py:510
  64.0 26.7 %all-to-all-start.2 = ((bf16[16,24,2048]{2,1,0:T(8,128)(2,1)}), bf16[16,24,2048]{2,1,0:T(8,128)(2,1)}, u32[]{:S(2)}, u32[]{:S(2)}) async-start(bf16[16,24,2048]{2,1,0:T(8,128)(2,1)} %bitcast.26), calls=%async_computation.2 | async-start | bytes 3145728 | tf_op jit(solution)/shard_map/all_to_all | solution.py:510
  90.7 28.3 %all-to-all-start.3 = ((bf16[16,24,2048]{2,1,0:T(8,128)(2,1)}), bf16[16,24,2048]{2,1,0:T(8,128)(2,1)}, u32[]{:S(2)}, u32[]{:S(2)}) async-start(bf16[16,24,2048]{2,1,0:T(8,128)(2,1)} %bitcast.25), calls=%async_computation.3 | async-start | bytes 3145728 | tf_op jit(solution)/shard_map/all_to_all | solution.py:510
  110.8 7.3 %collective-permute-start = (bf16[768,128]{1,0:T(8,128)(2,1)}, bf16[768,128]{1,0:T(8,128)(2,1)S(1)}, u32[]{:S(2)}, u32[]{:S(2)}) collective-permute-start(bf16[768,128]{1,0:T(8,128)(2,1)} %get-tuple-element.69), channel_id=1, source_target_pairs={{0,32},{16,48},{32,0},{48,16},{64,96},{80,112},{96,64},{112,80},{1... | collective-permute-start | bytes 589832 | tf_op jit(solution)/shard_map/ppermute | solution.py:497
  119.1 26.9 %all-to-all-start.4 = ((bf16[16,24,2048]{2,1,0:T(8,128)(2,1)}), bf16[16,24,2048]{2,1,0:T(8,128)(2,1)}, u32[]{:S(2)}, u32[]{:S(2)}) async-start(bf16[16,24,2048]{2,1,0:T(8,128)(2,1)} %bitcast.24), calls=%async_computation.4 | async-start | bytes 3145728 | tf_op jit(solution)/shard_map/all_to_all | solution.py:510
  129.0 7.7 %collective-permute-start.1 = (bf16[384,128]{1,0:T(8,128)(2,1)S(1)}, bf16[384,128]{1,0:T(8,128)(2,1)S(1)}, u32[]{:S(2)}, u32[]{:S(2)}) collective-permute-start(bf16[384,128]{1,0:T(8,128)(2,1)S(1)} %slice.37), channel_id=1, source_target_pairs={{0,64},{16,80},{32,96},{48,112},{64,0},{80,16},{96,32},{112,48},{1... | collective-permute-start | bytes 294920 | tf_op jit(solution)/shard_map/ppermute | solution.py:497
  136.7 8.1 %collective-permute-start.2 = (bf16[192,128]{1,0:T(8,128)(2,1)S(1)}, bf16[192,128]{1,0:T(8,128)(2,1)S(1)}, u32[]{:S(2)}, u32[]{:S(2)}) collective-permute-start(bf16[192,128]{1,0:T(8,128)(2,1)S(1)} %slice.49), channel_id=1, source_target_pairs={{0,128},{16,144},{32,160},{48,176},{64,192},{80,208},{96,224},{112... | collective-permute-start | bytes 147464 | tf_op jit(solution)/shard_map/ppermute | solution.py:497
  150.1 16.7 %all-to-all-start.5 = ((bf16[16,48,128]{2,1,0:T(8,128)(2,1)}), bf16[16,48,128]{2,1,0:T(8,128)(2,1)S(1)}, u32[]{:S(2)}, u32[]{:S(2)}) async-start(bf16[16,48,128]{2,1,0:T(8,128)(2,1)} %bitcast.28), calls=%async_computation.5 | async-start | bytes 393216 | tf_op jit(solution)/shard_map/all_to_all | solution.py:557
  153.6 8.2 %collective-permute-start.3 = (bf16[96,128]{1,0:T(8,128)(2,1)S(1)}, bf16[96,128]{1,0:T(8,128)(2,1)S(1)}, u32[]{:S(2)}, u32[]{:S(2)}) collective-permute-start(bf16[96,128]{1,0:T(8,128)(2,1)S(1)} %slice.43), channel_id=1, source_target_pairs={{0,16},{16,0},{32,48},{48,32},{64,80},{80,64},{96,112},{112,96},{1... | collective-permute-start | bytes 73736 | tf_op jit(solution)/shard_map/ppermute | solution.py:497
